TPU v7x, 32 devices: a whole 2x2x4 slice. The times are simulated.
32 devices in a mesh: energy: 8 (over y, x, core), slab: 4 (over z).
Axes of the slice: x: 2, y: 2, z: 4, core: 2. Of those that a mesh axis runs over, the one named last changes fastest.
Arguments:
- green_lesser: float32 [16, 4, 2, 128, 128], P('energy', 'slab'), may hold values from -6 to 6
- coupling: float32 [4, 4, 3, 2, 128, 128], P(None, 'slab'), may hold values from -0.375 to 0.375
- occupation: float32 [4], replicated, may hold values from 0.2 to 3
- shifts: int32 [4], replicated, may hold values from 1 to 2, as said below
- neighbours: int32 [4, 3], P('slab'), may hold values from 0 to 3, as said below
Outputs:
- self_energy: float32 [16, 4, 2, 128, 128], P('energy', 'slab')
Inputs may be any that keep to these rules, and one draw needn't show every extreme that they name: `shifts`: some mode's shift is 1 and some mode's shift is 2. `neighbours`: entry 0 of row i is max(i - 1, 0), entry 2 is min(i + 1, 3), entry 1 lies within one of i.
All inputs are finite; a program needn't handle non-finite values.
Results may differ from a plain program's by a relative error of at most 0.0001.
Values sent between devices are 32-bit elements; how exact they have to be, the bound alone decides.
No kernel may reach another device: no remote copies, remote signals or barrier semaphores. Data moves between devices by JAX's collectives and lax.ppermute only.
A program may use at most 64 MiB of HBM per device.

v0:
```python
import jax
import jax.numpy as jnp
from jax import lax
from jax.sharding import PartitionSpec as P


def padded_2(block, sides, width):
    for axis, dim in sides:
        count = lax.axis_size(axis)
        forward = [(i, i + 1) for i in range(count - 1)]
        backward = [(target, source) for source, target in forward]
        low = lax.ppermute(
            lax.slice_in_dim(block, block.shape[dim] - width, None, axis=dim), axis, forward
        )
        high = lax.ppermute(lax.slice_in_dim(block, 0, width, axis=dim), axis, backward)
        block = jnp.concatenate([low, block, high], axis=dim)
    return block


def passed_along(value, axis, steps):
    count = lax.axis_size(axis)
    leading, last = (max(0, -steps), min(count, count - steps))
    return lax.ppermute(value, axis, [(source, source + steps) for source in range(leading, last)])


def precise_matmul(first, second):
    return jnp.matmul(first, second, precision=lax.Precision.HIGHEST)


def complex_product(leading, trailing):
    lead_real, lead_imag = (leading[..., 0, :, :], leading[..., 1, :, :])
    trail_real, trail_imag = (trailing[..., 0, :, :], trailing[..., 1, :, :])
    real_part = precise_matmul(lead_real, trail_real) - precise_matmul(lead_imag, trail_imag)
    imag_part = precise_matmul(lead_real, trail_imag) + precise_matmul(lead_imag, trail_real)
    return jnp.stack([real_part, imag_part], axis=-3)


def adjoint_product(leading, trailing):
    lead_real, lead_imag = (leading[..., 0, :, :], leading[..., 1, :, :])
    trail_real = jnp.swapaxes(trailing[..., 0, :, :], -1, -2)
    trail_imag = jnp.swapaxes(trailing[..., 1, :, :], -1, -2)
    real_part = precise_matmul(lead_real, trail_real) + precise_matmul(lead_imag, trail_imag)
    imag_part = precise_matmul(lead_imag, trail_real) - precise_matmul(lead_real, trail_imag)
    return jnp.stack([real_part, imag_part], axis=-3)


def sandwich(couple, middle):
    return adjoint_product(complex_product(couple, middle), couple)


def shards(green_lesser, coupling, occupation, shifts, neighbours):
    energy_count = green_lesser.shape[0]
    block_count = green_lesser.shape[1]
    padded = padded_2(green_lesser, (("slab", 1),), 1)
    shifted = [passed_along(padded, "energy", offset_step) for offset_step in (1, -1)]
    gathered_blocks = jnp.concatenate([shifted[0], padded, shifted[1]], axis=0)
    position = neighbours - lax.axis_index("slab") * block_count + 1
    local_energy = jnp.arange(energy_count, dtype=jnp.int32) + energy_count
    summed = jnp.zeros_like(green_lesser)
    for mode_index in range(coupling.shape[0]):
        shift_now = shifts[mode_index]
        source = jnp.stack([local_energy + shift_now, local_energy - shift_now], axis=1)
        chosen = gathered_blocks[source[:, :, None, None], position[None, None, :, :]]
        couple = coupling[mode_index]
        weights = jnp.stack([occupation[mode_index] + 1.0, occupation[mode_index]])
        weighted = weights[0] * chosen[:, 0] + weights[1] * chosen[:, 1]
        summed = summed + jnp.sum(sandwich(couple[None], weighted), axis=2)
    return summed


def solution(mesh):
    placed = (
        P("energy", "slab", None, None, None),
        P(None, "slab", None, None, None, None),
        P(),
        P(),
        P("slab", None),
    )
    return jax.shard_map(
        shards,
        mesh=mesh,
        in_specs=placed,
        out_specs=P("energy", "slab", None, None, None),
        check_vma=False,
    )
```

profile of v0, /device:TPU:12, one launch (start us, length us, event | category | flops | bytes accessed | tf_op | source)
XLA Modules:
  0.0 111.2 jit_solution(16168244807886990456)
XLA Ops:
  0.0 3.6 %collective-permute-start = (f32[2,1,2,128,128]{4,3,2,1,0:T(8,128)}, f32[2,1,2,128,128]{4,3,2,1,0:T(8,128)S(1)}, u32[]{:S(2)}, u32[]{:S(2)}) collective-permute-start(f32[2,1,2,128,128]{4,3,2,1,0:T(8,128)} %param.5), channel_id=1, source_target_pairs={{0,1},{1,2},{2,3},{4,5},{5,6},{6,7},{8,9},{9,10},{10,11},{12,13},{... | collective-permute-start | bytes 786440 | tf_op jit(solution)/shard_map/ppermute | solution.py:12
  3.6 2.4 %collective-permute-start.1 = (f32[2,1,2,128,128]{4,3,2,1,0:T(8,128)}, f32[2,1,2,128,128]{4,3,2,1,0:T(8,128)S(1)}, u32[]{:S(2)}, u32[]{:S(2)}) collective-permute-start(f32[2,1,2,128,128]{4,3,2,1,0:T(8,128)} %param.5), channel_id=1, source_target_pairs={{1,0},{2,1},{3,2},{5,4},{6,5},{7,6},{9,8},{10,9},{11,10},{13,12},{... | collective-permute-start | bytes 786440 | tf_op jit(solution)/shard_map/ppermute | solution.py:15
  18.0 2.2 %collective-permute-start.3 = (f32[2,3,2,128,128]{4,3,2,1,0:T(8,128)S(1)}, f32[2,3,2,128,128]{4,3,2,1,0:T(8,128)S(1)}, u32[]{:S(2)}, u32[]{:S(2)}) collective-permute-start(f32[2,3,2,128,128]{4,3,2,1,0:T(8,128)S(1)} %constant_dynamic-update-slice_fusion), channel_id=1, source_target_pairs={{4,0},{8,4},{12,8},{16,12},{20,16},{24,20},{28,24},{5,1},{9,5},{13... | collective-permute-start | bytes 2359304 | tf_op jit(solution)/shard_map/ppermute | solution.py:23
  20.2 2.1 %collective-permute-start.2 = (f32[2,3,2,128,128]{4,3,2,1,0:T(8,128)S(1)}, f32[2,3,2,128,128]{4,3,2,1,0:T(8,128)}, u32[]{:S(2)}, u32[]{:S(2)}) collective-permute-start(f32[2,3,2,128,128]{4,3,2,1,0:T(8,128)S(1)} %constant_dynamic-update-slice_fusion), channel_id=1, source_target_pairs={{0,4},{4,8},{8,12},{12,16},{16,20},{20,24},{24,28},{1,5},{5,9},{9,... | collective-permute-start | bytes 2359304 | tf_op jit(solution)/shard_map/ppermute | solution.py:23
  23.2 12.3 %collective-permute-done.3 = f32[2,3,2,128,128]{4,3,2,1,0:T(8,128)S(1)} collective-permute-done((f32[2,3,2,128,128]{4,3,2,1,0:T(8,128)S(1)}, f32[2,3,2,128,128]{4,3,2,1,0:T(8,128)S(1)}, u32[]{:S(2)}, u32[]{:S(2)}) %collective-permute-start.3) | collective-permute-done | bytes 786464 | tf_op jit(solution)/shard_map/ppermute | solution.py:23
  36.4 3.4 %collective-permute-done.2 = f32[2,3,2,128,128]{4,3,2,1,0:T(8,128)} collective-permute-done((f32[2,3,2,128,128]{4,3,2,1,0:T(8,128)S(1)}, f32[2,3,2,128,128]{4,3,2,1,0:T(8,128)}, u32[]{:S(2)}, u32[]{:S(2)}) %collective-permute-start.2) | collective-permute-done | bytes 786464 | tf_op jit(solution)/shard_map/ppermute | solution.py:23
  41.3 1.9 %gather_fusion.3 = f32[12,2,128,128]{3,2,1,0:T(8,128)} fusion(f32[6,3,2,128,128]{4,3,2,1,0:T(8,128)S(1)} %pad_maximum_fusion, s32[12]{0:T(128)S(1)} %reshape.427), kind=kCustom, calls=%fused_computation.3 | custom fusion | bytes 3145824 | tf_op jit(solution)/shard_map/gather | solution.py:63
  43.2 2.4 %fusion.127 = (f32[2,1,1,3,2,128,128]{6,5,4,3,1,0,2:T(8,128)}, f32[2,1,1,3,2,128,128]{6,5,4,3,1,0,2:T(8,128)S(1)}) fusion(f32[2,2,1,3,2,128,128]{6,5,4,3,1,0,2:T(8,128)} %bitcast.337), kind=kLoop, calls=%fused_computation.186 | loop fusion | bytes 3145728 | tf_op jit(solution)/shard_map/slice | solution.py:66
  45.6 2.3 %copy.227 = f32[2,1,1,3,2,128,128]{5,6,0,3,4,2,1:T(8,128)} copy(f32[2,1,1,3,2,128,128]{6,5,4,3,1,0,2:T(8,128)} %get-tuple-element.11) | data formatting | bytes 1572864
  49.0 2.1 %add_bitcast_fusion = f32[2,1,3,2,128,128]{4,5,0,2,3,1:T(8,128)S(1)} fusion(f32[2,1,1,3,2,128,128]{5,6,0,3,4,2,1:T(8,128)} %copy.228, f32[2,1,1,3,2,128,128]{5,6,0,3,4,2,1:T(8,128)} %copy.227, f32[]{:T(128)} %bitcast.112, f32[]{:T(128)S(6)} %add.393), kind=kLoop, calls=%fused_computation.41 | loop fusion | flops 589824 | bytes 2359304 | tf_op jit(solution)/shard_map/add | solution.py:66
  51.2 2.2 %fusion.23 = f32[3,2,128,128]{3,2,1,0:T(8,128)} fusion(f32[2,1,3,2,128,128]{4,5,0,2,3,1:T(8,128)S(1)} %add_bitcast_fusion, f32[4,1,3,2,128,128]{5,4,3,2,1,0:T(8,128)} %param.6), kind=kOutput, calls=%fused_computation.60 | convolution fusion | flops 150994944 | bytes 983040 | tf_op jit(solution)/shard_map/dot_general | solution.py:27
  54.8 1.9 %gather_fusion.2 = f32[12,2,128,128]{3,2,1,0:T(8,128)} fusion(f32[6,3,2,128,128]{4,3,2,1,0:T(8,128)S(1)} %pad_maximum_fusion, s32[12]{0:T(128)S(1)} %reshape.419), kind=kCustom, calls=%fused_computation.2 | custom fusion | bytes 3145824 | tf_op jit(solution)/shard_map/gather | solution.py:63
  56.6 2.7 %fusion.126 = (f32[2,1,1,3,2,128,128]{6,5,4,3,1,0,2:T(8,128)}, f32[2,1,1,3,2,128,128]{6,5,4,3,1,0,2:T(8,128)}) fusion(f32[2,2,1,3,2,128,128]{6,5,4,3,1,0,2:T(8,128)} %bitcast.338), kind=kLoop, calls=%fused_computation.185 | loop fusion | bytes 3145728 | tf_op jit(solution)/shard_map/slice | solution.py:66
  59.4 2.3 %copy.223 = f32[2,1,1,3,2,128,128]{5,6,0,3,4,2,1:T(8,128)} copy(f32[2,1,1,3,2,128,128]{6,5,4,3,1,0,2:T(8,128)} %get-tuple-element.9) | data formatting | bytes 1572864
  61.6 2.3 %copy.224 = f32[2,1,1,3,2,128,128]{5,6,0,3,4,2,1:T(8,128)} copy(f32[2,1,1,3,2,128,128]{6,5,4,3,1,0,2:T(8,128)} %get-tuple-element.10) | data formatting | bytes 1572864
  63.9 2.1 %add_bitcast_fusion.1 = f32[2,1,3,2,128,128]{4,5,0,2,3,1:T(8,128)S(1)} fusion(f32[2,1,1,3,2,128,128]{5,6,0,3,4,2,1:T(8,128)} %copy.224, f32[2,1,1,3,2,128,128]{5,6,0,3,4,2,1:T(8,128)} %copy.223, f32[]{:T(128)} %bitcast.75, f32[]{:T(128)S(6)} %add.382), kind=kLoop, calls=%fused_computation.42 | loop fusion | flops 589824 | bytes 2359304 | tf_op jit(solution)/shard_map/add | solution.py:66
  66.1 2.4 %fusion.21 = f32[3,2,128,128]{3,2,1,0:T(8,128)} fusion(f32[2,1,3,2,128,128]{4,5,0,2,3,1:T(8,128)S(1)} %add_bitcast_fusion.1, f32[4,1,3,2,128,128]{5,4,3,2,1,0:T(8,128)} %param.6), kind=kOutput, calls=%fused_computation.58 | convolution fusion | flops 150994944 | bytes 983040 | tf_op jit(solution)/shard_map/dot_general | solution.py:27
  68.5 2.2 %fusion.20 = f32[3,2,128,128]{3,2,1,0:T(8,128)} fusion(f32[2,1,3,2,128,128]{4,5,0,2,3,1:T(8,128)S(1)} %add_bitcast_fusion.1, f32[4,1,3,2,128,128]{5,4,3,2,1,0:T(8,128)} %param.6), kind=kOutput, calls=%fused_computation.57 | convolution fusion | flops 150994944 | bytes 983040 | tf_op jit(solution)/shard_map/dot_general | solution.py:27
  72.6 2.7 %fusion.125 = (f32[2,1,1,3,2,128,128]{6,5,4,3,1,0,2:T(8,128)}, f32[2,1,1,3,2,128,128]{6,5,4,3,1,0,2:T(8,128)}) fusion(f32[2,2,1,3,2,128,128]{6,5,4,3,1,0,2:T(8,128)} %bitcast.339), kind=kLoop, calls=%fused_computation.184 | loop fusion | bytes 3145728 | tf_op jit(solution)/shard_map/slice | solution.py:66
  75.2 2.3 %copy.215 = f32[2,1,1,3,2,128,128]{5,6,0,3,4,2,1:T(8,128)} copy(f32[2,1,1,3,2,128,128]{6,5,4,3,1,0,2:T(8,128)} %get-tuple-element.7) | data formatting | bytes 1572864
  77.5 2.3 %copy.216 = f32[2,1,1,3,2,128,128]{5,6,0,3,4,2,1:T(8,128)} copy(f32[2,1,1,3,2,128,128]{6,5,4,3,1,0,2:T(8,128)} %get-tuple-element.8) | data formatting | bytes 1572864
  79.8 2.1 %add_bitcast_fusion.3 = f32[2,1,3,2,128,128]{4,5,0,2,3,1:T(8,128)S(1)} fusion(f32[2,1,1,3,2,128,128]{5,6,0,3,4,2,1:T(8,128)} %copy.216, f32[2,1,1,3,2,128,128]{5,6,0,3,4,2,1:T(8,128)} %copy.215, f32[]{:T(128)} %bitcast, f32[]{:T(128)S(6)} %add.358), kind=kLoop, calls=%fused_computation.44 | loop fusion | flops 589824 | bytes 2359304 | tf_op jit(solution)/shard_map/add | solution.py:66
  81.9 2.4 %fusion.17 = f32[3,2,128,128]{3,2,1,0:T(8,128)} fusion(f32[2,1,3,2,128,128]{4,5,0,2,3,1:T(8,128)S(1)} %add_bitcast_fusion.3, f32[4,1,3,2,128,128]{5,4,3,2,1,0:T(8,128)} %param.6), kind=kOutput, calls=%fused_computation.54 | convolution fusion | flops 150994944 | bytes 983040 | tf_op jit(solution)/shard_map/dot_general | solution.py:27
  84.4 2.1 %fusion.16 = f32[3,2,128,128]{3,2,1,0:T(8,128)} fusion(f32[2,1,3,2,128,128]{4,5,0,2,3,1:T(8,128)S(1)} %add_bitcast_fusion.3, f32[4,1,3,2,128,128]{5,4,3,2,1,0:T(8,128)} %param.6), kind=kOutput, calls=%fused_computation.53 | convolution fusion | flops 150994944 | bytes 983040 | tf_op jit(solution)/shard_map/dot_general | solution.py:27
  (97 shorter events, 41.2 us)
Async XLA Ops:
  0.0 22.5 %copy-start.11 = (s32[1,3]{1,0:T(1,128)S(1)}, s32[1,3]{1,0:T(1,128)}, u32[]{:S(2)}) copy-start(s32[1,3]{1,0:T(1,128)} %param.9) | copy-start | bytes 40
  0.0 16.9 %collective-permute-start = (f32[2,1,2,128,128]{4,3,2,1,0:T(8,128)}, f32[2,1,2,128,128]{4,3,2,1,0:T(8,128)S(1)}, u32[]{:S(2)}, u32[]{:S(2)}) collective-permute-start(f32[2,1,2,128,128]{4,3,2,1,0:T(8,128)} %param.5), channel_id=1, source_target_pairs={{0,1},{1,2},{2,3},{4,5},{5,6},{6,7},{8,9},{9,10},{10,11},{12,13},{... | collective-permute-start | bytes 786440 | tf_op jit(solution)/shard_map/ppermute | solution.py:12
  3.6 14.3 %collective-permute-start.1 = (f32[2,1,2,128,128]{4,3,2,1,0:T(8,128)}, f32[2,1,2,128,128]{4,3,2,1,0:T(8,128)S(1)}, u32[]{:S(2)}, u32[]{:S(2)}) collective-permute-start(f32[2,1,2,128,128]{4,3,2,1,0:T(8,128)} %param.5), channel_id=1, source_target_pairs={{1,0},{2,1},{3,2},{5,4},{6,5},{7,6},{9,8},{10,9},{11,10},{13,12},{... | collective-permute-start | bytes 786440 | tf_op jit(solution)/shard_map/ppermute | solution.py:15
  18.0 17.5 %collective-permute-start.3 = (f32[2,3,2,128,128]{4,3,2,1,0:T(8,128)S(1)}, f32[2,3,2,128,128]{4,3,2,1,0:T(8,128)S(1)}, u32[]{:S(2)}, u32[]{:S(2)}) collective-permute-start(f32[2,3,2,128,128]{4,3,2,1,0:T(8,128)S(1)} %constant_dynamic-update-slice_fusion), channel_id=1, source_target_pairs={{4,0},{8,4},{12,8},{16,12},{20,16},{24,20},{28,24},{5,1},{9,5},{13... | collective-permute-start | bytes 2359304 | tf_op jit(solution)/shard_map/ppermute | solution.py:23
  20.2 19.6 %collective-permute-start.2 = (f32[2,3,2,128,128]{4,3,2,1,0:T(8,128)S(1)}, f32[2,3,2,128,128]{4,3,2,1,0:T(8,128)}, u32[]{:S(2)}, u32[]{:S(2)}) collective-permute-start(f32[2,3,2,128,128]{4,3,2,1,0:T(8,128)S(1)} %constant_dynamic-update-slice_fusion), channel_id=1, source_target_pairs={{0,4},{4,8},{8,12},{12,16},{16,20},{20,24},{24,28},{1,5},{5,9},{9,... | collective-permute-start | bytes 2359304 | tf_op jit(solution)/shard_map/ppermute | solution.py:23
  35.5 0.9 copy-start.10
  66.1 2.4 %copy-start.1 = (f32[2,1,3,2,128,128]{4,5,0,2,3,1:T(8,128)}, f32[2,1,3,2,128,128]{4,5,0,2,3,1:T(8,128)S(1)}, u32[]{:S(2)}) copy-start(f32[2,1,3,2,128,128]{4,5,0,2,3,1:T(8,128)S(1)} %add_bitcast_fusion.1) | copy-start | bytes 2359300
  81.9 2.4 %copy-start.3 = (f32[2,1,3,2,128,128]{4,5,0,2,3,1:T(8,128)}, f32[2,1,3,2,128,128]{4,5,0,2,3,1:T(8,128)S(1)}, u32[]{:S(2)}) copy-start(f32[2,1,3,2,128,128]{4,5,0,2,3,1:T(8,128)S(1)} %add_bitcast_fusion.3) | copy-start | bytes 2359300
  90.4 1.4 %copy-start = (f32[4,1,3,2,128,128]{5,4,3,2,1,0:T(8,128)S(1)}, f32[4,1,3,2,128,128]{5,4,3,2,1,0:T(8,128)}, u32[]{:S(2)}) copy-start(f32[4,1,3,2,128,128]{5,4,3,2,1,0:T(8,128)} %param.6) | copy-start | bytes 4718596
  91.8 1.0 copy-start.5
  95.4 1.7 %copy-start.2 = (f32[2,1,3,2,128,128]{4,5,0,2,3,1:T(8,128)S(1)}, f32[2,1,3,2,128,128]{4,5,0,2,3,1:T(8,128)}, u32[]{:S(2)}) copy-start(f32[2,1,3,2,128,128]{4,5,0,2,3,1:T(8,128)} %copy-done.1) | copy-start | bytes 2359300
  95.5 1.7 %copy-start.7 = (f32[3,2,128,128]{3,2,1,0:T(8,128)S(1)}, f32[3,2,128,128]{3,2,1,0:T(8,128)}, u32[]{:S(2)}) copy-start(f32[3,2,128,128]{3,2,1,0:T(8,128)} %fusion.21) | copy-start | bytes 1179652
  96.3 2.3 %copy-start.6 = (f32[3,2,128,128]{3,2,1,0:T(8,128)S(1)}, f32[3,2,128,128]{3,2,1,0:T(8,128)}, u32[]{:S(2)}) copy-start(f32[3,2,128,128]{3,2,1,0:T(8,128)} %fusion.20) | copy-start | bytes 1179652
  100.0 1.7 %copy-start.4 = (f32[2,1,3,2,128,128]{4,5,0,2,3,1:T(8,128)S(1)}, f32[2,1,3,2,128,128]{4,5,0,2,3,1:T(8,128)}, u32[]{:S(2)}) copy-start(f32[2,1,3,2,128,128]{4,5,0,2,3,1:T(8,128)} %copy-done.3) | copy-start | bytes 2359300
  100.0 1.7 %copy-start.9 = (f32[3,2,128,128]{3,2,1,0:T(8,128)S(1)}, f32[3,2,128,128]{3,2,1,0:T(8,128)}, u32[]{:S(2)}) copy-start(f32[3,2,128,128]{3,2,1,0:T(8,128)} %fusion.17) | copy-start | bytes 1179652
  100.8 2.2 %copy-start.8 = (f32[3,2,128,128]{3,2,1,0:T(8,128)S(1)}, f32[3,2,128,128]{3,2,1,0:T(8,128)}, u32[]{:S(2)}) copy-start(f32[3,2,128,128]{3,2,1,0:T(8,128)} %fusion.16) | copy-start | bytes 1179652
where the time goes:
time: 112 us; the launch traced here: 111 us
  local copies, waits for them, and re-layouts  36.6 us (33%)
  matrix products  30.8 us (28%)
  waiting for transfers between devices  15.7 us (14%)
  other arithmetic  14.5 us (13%)
  starting transfers between devices  10.3 us (9%)
  between operations  3.27 us (3%)
    dot_general x32, matrix products, precise_matmul(): return jnp.matmul(first, second, precision=lax.Precision.HIGHEST)  30.8 us
    ppermute x2, waiting for transfers between devices, passed_along(): lax.ppermute(value, axis, [(source, source + steps) for source in range(l...  15.7 us
    unnamed x34, local copies, waits for them, and re-layouts  15.6 us
    slice x4, local copies, waits for them, and re-layouts, shards(): weighted = weights[0] * chosen[:, 0] + weights[1] * chosen[:, 1]  9.26 us
    gather x4, local copies, waits for them, and re-layouts, shards(): gathered_blocks[source[:, :, None, None], position[None, None, :, :]]  7.42 us
    add x4, other arithmetic, shards(): weighted = weights[0] * chosen[:, 0] + weights[1] * chosen[:, 1]  7.28 us
    ppermute x2, starting transfers between devices, passed_along(): lax.ppermute(value, axis, [(source, source + steps) for source in range(l...  4.33 us
    ppermute x1, starting transfers between devices, padded_2(): lax.ppermute(lax.slice_in_dim(block, block.shape[dim] - width, None, axis...  3.61 us
  transfers between devices with their start and end apart: 4, of which 2 were waited for; matrix products, arithmetic and copies ran while one was open for 9% of the time, Pallas kernels for 0%

commit v1 on v0

v1 whole, which is shorter than its diff:
```python
import functools

import jax
import jax.numpy as jnp
from jax import lax
from jax.experimental import pallas as pl
from jax.experimental.pallas import tpu as pltpu
from jax.sharding import PartitionSpec as P


def neighbour_pairs(mesh, axis, other, odd):
    count, count_other = mesh.shape[axis], mesh.shape[other]
    axes = tuple(mesh.axis_names)
    pairs = []
    for here in range(count):
        there = here ^ 1 if not odd else ((here + 1) ^ 1) - 1
        for side in range(count_other):
            inside = 0 <= there < count
            source = {axis: here, other: side}
            target = {axis: there, other: side} if inside else {axis: here, other: side ^ 1}
            if target[other] < count_other:
                flat = [at[axes[0]] * mesh.shape[axes[1]] + at[axes[1]] for at in (source, target)]
                pairs.append((flat[0], flat[1]))
    return axes, pairs


def split(value):
    high = value.astype(jnp.bfloat16)
    return high, (value - high.astype(jnp.float32)).astype(jnp.bfloat16)


def product(lead_high, lead_low, trail_high, trail_low, contract):
    dims = (((1,), (contract,)), ((), ()))
    dot = functools.partial(lax.dot_general, dimension_numbers=dims, preferred_element_type=jnp.float32)
    return dot(lead_high, trail_high) + (dot(lead_low, trail_high) + dot(lead_high, trail_low))


def sandwich_kernel(
    shifts_ref, occupation_ref, neighbours_ref, own_ref, even_ref, odd_ref, couple_ref,
    stay_ref, give_even_ref, give_odd_ref,
    embed_high, embed_low, lead_high, lead_low, back_high, back_low, total,
):
    energies, _, _, size, _ = own_ref.shape
    modes, _, blocks = couple_ref.shape[:3]
    here, place = lax.axis_index("slab"), lax.axis_index("energy")
    for source, ref in enumerate((own_ref, even_ref, odd_ref)):
        for energy in range(energies):
            real_high, real_low = split(ref[energy, 0, 0])
            imag_high, imag_low = split(ref[energy, 0, 1])
            for embed, real, imag in ((embed_high, real_high, imag_high), (embed_low, real_low, imag_low)):
                embed[source, energy, :size, :size] = real
                embed[source, energy, :size, size:] = imag
                embed[source, energy, size:, :size] = -imag
                embed[source, energy, size:, size:] = real
    for block in range(blocks):
        for mode in range(modes):
            real_high, real_low = split(couple_ref[mode, 0, block, 0])
            imag_high, imag_low = split(couple_ref[mode, 0, block, 1])
            rows = slice(mode * size, (mode + 1) * size)
            columns = slice(block * 2 * size, block * 2 * size + size)
            others = slice(block * 2 * size + size, (block + 1) * 2 * size)
            for lead, back, real, imag in (
                (lead_high, back_high, real_high, imag_high),
                (lead_low, back_low, real_low, imag_low),
            ):
                lead[block, rows, :size] = real
                lead[block, rows, size:] = imag
                back[mode, :size, columns] = real
                back[mode, :size, others] = imag
                back[mode, size:, columns] = -imag
                back[mode, size:, others] = real
    total[...] = jnp.zeros_like(total)
    middles = [[] for _ in range(energies)]
    for block in range(blocks):
        offset = neighbours_ref[0, block] - here
        ahead = 1 - 2 * lax.rem(here, 2)
        source = jnp.where(offset == 0, 0, jnp.where(offset == ahead, 1, 2))
        for energy in range(energies):
            middles[energy].append(
                product(
                    lead_high[block], lead_low[block],
                    embed_high[source, energy], embed_low[source, energy], 0,
                )
            )
    for mode in range(modes):
        shift, number = shifts_ref[mode], occupation_ref[mode]
        rows = slice(mode * size, (mode + 1) * size)
        stacked = jnp.concatenate(
            [jnp.concatenate([part[rows] for part in middles[energy]], axis=1) for energy in range(energies)], axis=0
        )
        high, low = split(stacked)
        result = product(high, low, back_high[mode], back_low[mode], 1)
        for energy in range(energies):
            part = result[energy * size : (energy + 1) * size]
            total[energy + energies - shift] += (number + 1.0) * part
            total[energy + energies + shift] += number * part
    left_first = lax.rem(place, 2) == 1
    to_even = jnp.where(left_first, 0, 2 * energies)
    to_odd = jnp.where(left_first, 2 * energies, 0)
    for ref, first in ((stay_ref, energies), (give_even_ref, to_even), (give_odd_ref, to_odd)):
        for energy in range(energies):
            value = total[first + energy]
            ref[energy, 0, 0] = value[:, :size]
            ref[energy, 0, 1] = value[:, size:]


def sum_kernel(ends, stay_ref, got_even_ref, got_odd_ref, out_ref):
    place = lax.axis_index("energy")
    inside = jnp.logical_and(place != 0, place != ends)
    out_ref[...] = stay_ref[...] + got_even_ref[...] + jnp.where(inside, got_odd_ref[...], 0.0)


def shards(mesh, green_lesser, coupling, occupation, shifts, neighbours):
    energies, _, _, size, _ = green_lesser.shape
    modes, _, blocks = coupling.shape[:3]
    swap = lambda value, axis, other, odd: lax.ppermute(value, *neighbour_pairs(mesh, axis, other, odd))
    even = swap(green_lesser, "slab", "energy", False)
    odd = swap(green_lesser, "slab", "energy", True)
    whole = pl.BlockSpec(memory_space=pltpu.VMEM)
    scalar = pl.BlockSpec(memory_space=pltpu.SMEM)
    block = jax.ShapeDtypeStruct(green_lesser.shape, jnp.float32)
    stay, give_even, give_odd = pl.pallas_call(
        sandwich_kernel,
        out_shape=[block] * 3,
        in_specs=[scalar] * 3 + [whole] * 4,
        out_specs=[whole] * 3,
        scratch_shapes=[pltpu.VMEM((3, energies, 2 * size, 2 * size), jnp.bfloat16)] * 2
        + [pltpu.VMEM((blocks, modes * size, 2 * size), jnp.bfloat16)] * 2
        + [pltpu.VMEM((modes, 2 * size, blocks * 2 * size), jnp.bfloat16)] * 2
        + [pltpu.VMEM((3 * energies, size, 2 * size), jnp.float32)],
        compiler_params=pltpu.CompilerParams(vmem_limit_bytes=32 << 20),
    )(shifts, occupation, neighbours, green_lesser, even, odd, coupling)
    got_even = swap(give_even, "energy", "slab", False)
    got_odd = swap(give_odd, "energy", "slab", True)
    return pl.pallas_call(
        functools.partial(sum_kernel, mesh.shape["energy"] - 1),
        out_shape=block,
        in_specs=[whole] * 3,
        out_specs=whole,
    )(stay, got_even, got_odd)


def solution(mesh):
    placed = (
        P("energy", "slab", None, None, None),
        P(None, "slab", None, None, None, None),
        P(),
        P(),
        P("slab", None),
    )
    return jax.shard_map(
        functools.partial(shards, mesh),
        mesh=mesh,
        in_specs=placed,
        out_specs=P("energy", "slab", None, None, None),
        check_vma=False,
    )
```

time: 112 us -> 30.8 us (0.28)
  the two profiles are of different devices: /device:TPU:12 before, /device:TPU:19 now
where the time goes in v1:
time: 30.8 us; the launch traced here: 30.6 us
  waiting for transfers between devices  14.8 us (48%)
  Pallas kernels  5.74 us (19%)
  local copies, waits for them, and re-layouts  5.71 us (19%)
  starting transfers between devices  4.26 us (14%)
    ppermute x4, waiting for transfers between devices, shards(): lax.ppermute(value, *neighbour_pairs(mesh, axis, other, odd))  14.8 us
    unnamed x16, local copies, waits for them, and re-layouts  5.71 us
    ppermute x4, starting transfers between devices, shards(): lax.ppermute(value, *neighbour_pairs(mesh, axis, other, odd))  4.26 us
    pallas_call x1, Pallas kernels, shards(): pl.pallas_call(sandwich_kernel, out_shape=[block] * 3, in_specs=[scalar]...  3.89 us
    pallas_call x1, Pallas kernels, shards(): pl.pallas_call(functools.partial(sum_kernel, mesh.shape['energy'] - 1), o...  1.85 us
  transfers between devices with their start and end apart: 4, of which 4 were waited for; matrix products, arithmetic and copies ran while one was open for 0% of the time, Pallas kernels for 0%

profile of v1, /device:TPU:19, one launch (start us, length us, event | category | flops | bytes accessed | tf_op | source)
XLA Modules:
  0.0 30.6 jit_solution(14314727228265754432)
XLA Ops:
  0.0 1.3 %collective-permute-start = (f32[2,1,2,128,128]{4,3,2,1,0:T(8,128)}, f32[2,1,2,128,128]{4,3,2,1,0:T(8,128)S(1)}, u32[]{:S(2)}, u32[]{:S(2)}) collective-permute-start(f32[2,1,2,128,128]{4,3,2,1,0:T(8,128)} %own_ref.1), channel_id=1, source_target_pairs={{0,1},{4,5},{8,9},{12,13},{16,17},{20,21},{24,25},{28,29},{1,0},{5... | collective-permute-start | bytes 786440 | tf_op jit(solution)/shard_map/ppermute | solution.py:116
  1.3 0.0 collective-permute-start.1
  1.3 6.1 %collective-permute-done.even_ref = f32[2,1,2,128,128]{4,3,2,1,0:T(8,128)S(1)} collective-permute-done((f32[2,1,2,128,128]{4,3,2,1,0:T(8,128)}, f32[2,1,2,128,128]{4,3,2,1,0:T(8,128)S(1)}, u32[]{:S(2)}, u32[]{:S(2)}) %collective-permute-start) | collective-permute-done | bytes 262176 | tf_op jit(solution)/shard_map/ppermute | solution.py:116
  7.4 1.0 %collective-permute-done.1.odd_ref = f32[2,1,2,128,128]{4,3,2,1,0:T(8,128)S(1)} collective-permute-done((f32[2,1,2,128,128]{4,3,2,1,0:T(8,128)}, f32[2,1,2,128,128]{4,3,2,1,0:T(8,128)S(1)}, u32[]{:S(2)}, u32[]{:S(2)}) %collective-permute-start.1) | collective-permute-done | bytes 262176 | tf_op jit(solution)/shard_map/ppermute | solution.py:116
  8.4 0.0 copy-start
  8.4 1.4 %copy-done = f32[4,1,3,2,128,128]{5,4,3,2,1,0:T(8,128)S(1)} copy-done((f32[4,1,3,2,128,128]{5,4,3,2,1,0:T(8,128)S(1)}, f32[4,1,3,2,128,128]{5,4,3,2,1,0:T(8,128)}, u32[]{:S(2)}) %copy-start) | copy-done | bytes 1572888
  9.8 0.0 copy-start.1
  9.8 0.9 %copy-done.1 = f32[2,1,2,128,128]{4,3,2,1,0:T(8,128)S(1)} copy-done((f32[2,1,2,128,128]{4,3,2,1,0:T(8,128)S(1)}, f32[2,1,2,128,128]{4,3,2,1,0:T(8,128)}, u32[]{:S(2)}) %copy-start.1) | copy-done | bytes 262168
  10.7 0.0 copy-start.3
  10.7 0.7 %copy-done.3 = s32[4]{0:T(128)S(1)} copy-done((s32[4]{0:T(128)S(1)}, s32[4]{0:T(128)}, u32[]{:S(2)}) %copy-start.3) | copy-done | bytes 40
  11.4 0.0 copy-start.4
  11.4 0.7 %copy-done.4 = f32[4]{0:T(128)S(1)} copy-done((f32[4]{0:T(128)S(1)}, f32[4]{0:T(128)}, u32[]{:S(2)}) %copy-start.4) | copy-done | bytes 40
  12.0 0.0 copy-start.5
  12.0 0.7 %copy-done.5 = s32[1,3]{1,0:T(1,128)S(1)} copy-done((s32[1,3]{1,0:T(1,128)S(1)}, s32[1,3]{1,0:T(1,128)}, u32[]{:S(2)}) %copy-start.5) | copy-done | bytes 36
  12.7 3.9 %shard_map.55 = (f32[2,1,2,128,128]{4,3,2,1,0:T(8,128)S(1)}, f32[2,1,2,128,128]{4,3,2,1,0:T(8,128)S(1)}, f32[2,1,2,128,128]{4,3,2,1,0:T(8,128)S(1)}) custom-call(s32[4]{0:T(128)S(1)} %copy-done.3, f32[4]{0:T(128)S(1)} %copy-done.4, s32[1,3]{1,0:T(1,128)S(1)} %copy-done.5, f32[2,1,2,128,128]{4,3,2,1,0:T(8,128)S(1)} %copy-done.1, ...), custom_call_target="tpu_custom_call" | custom-call | tf_op jit(solution)/shard_map/pallas_call | solution.py:122
  16.6 0.0 copy-start.2
  16.6 0.7 %copy-done.2 = f32[2,1,2,128,128]{4,3,2,1,0:T(8,128)} copy-done((f32[2,1,2,128,128]{4,3,2,1,0:T(8,128)}, f32[2,1,2,128,128]{4,3,2,1,0:T(8,128)S(1)}, u32[]{:S(2)}) %copy-start.2) | copy-done | bytes 262168
  17.3 1.9 %collective-permute-start.2 = (f32[2,1,2,128,128]{4,3,2,1,0:T(8,128)S(1)}, f32[2,1,2,128,128]{4,3,2,1,0:T(8,128)S(1)}, u32[]{:S(2)}, u32[]{:S(2)}) collective-permute-start(f32[2,1,2,128,128]{4,3,2,1,0:T(8,128)S(1)} %get-tuple-element.9), channel_id=1, source_target_pairs={{0,4},{1,5},{2,6},{3,7},{4,0},{5,1},{6,2},{7,3},{8,12},{9,13},{10,... | collective-permute-start | bytes 786440 | tf_op jit(solution)/shard_map/ppermute | solution.py:116
  19.2 1.1 %collective-permute-start.3 = (f32[2,1,2,128,128]{4,3,2,1,0:T(8,128)S(1)}, f32[2,1,2,128,128]{4,3,2,1,0:T(8,128)S(1)}, u32[]{:S(2)}, u32[]{:S(2)}) collective-permute-start(f32[2,1,2,128,128]{4,3,2,1,0:T(8,128)S(1)} %get-tuple-element.10), channel_id=1, source_target_pairs={{0,1},{1,0},{2,3},{3,2},{4,8},{5,9},{6,10},{7,11},{8,4},{9,5},{10,... | collective-permute-start | bytes 786440 | tf_op jit(solution)/shard_map/ppermute | solution.py:116
  20.3 0.1 collective-permute-done.2.got_even_ref
  20.3 7.7 %collective-permute-done.3.got_odd_ref = f32[2,1,2,128,128]{4,3,2,1,0:T(8,128)S(1)} collective-permute-done((f32[2,1,2,128,128]{4,3,2,1,0:T(8,128)S(1)}, f32[2,1,2,128,128]{4,3,2,1,0:T(8,128)S(1)}, u32[]{:S(2)}, u32[]{:S(2)}) %collective-permute-start.3) | collective-permute-done | bytes 262176 | tf_op jit(solution)/shard_map/ppermute | solution.py:116
  28.0 0.0 copy-done.6
  28.0 0.7 %copy-done.7 = f32[2,1,2,128,128]{4,3,2,1,0:T(8,128)} copy-done((f32[2,1,2,128,128]{4,3,2,1,0:T(8,128)}, f32[2,1,2,128,128]{4,3,2,1,0:T(8,128)S(1)}, u32[]{:S(2)}) %copy-start.7) | copy-done | bytes 262168
  28.7 1.8 %shard_map.56 = f32[2,1,2,128,128]{4,3,2,1,0:T(8,128)} custom-call(f32[2,1,2,128,128]{4,3,2,1,0:T(8,128)} %copy-done.2, f32[2,1,2,128,128]{4,3,2,1,0:T(8,128)} %copy-done.6, f32[2,1,2,128,128]{4,3,2,1,0:T(8,128)} %copy-done.7), custom_call_target="tpu_custom_call" | custom-call | tf_op jit(solution)/shard_map/pallas_call | solution.py:135
  (2 shorter events, 0.0 us)
Async XLA Ops:
  0.0 7.4 %collective-permute-start = (f32[2,1,2,128,128]{4,3,2,1,0:T(8,128)}, f32[2,1,2,128,128]{4,3,2,1,0:T(8,128)S(1)}, u32[]{:S(2)}, u32[]{:S(2)}) collective-permute-start(f32[2,1,2,128,128]{4,3,2,1,0:T(8,128)} %own_ref.1), channel_id=1, source_target_pairs={{0,1},{4,5},{8,9},{12,13},{16,17},{20,21},{24,25},{28,29},{1,0},{5... | collective-permute-start | bytes 786440 | tf_op jit(solution)/shard_map/ppermute | solution.py:116
  1.3 7.1 %collective-permute-start.1 = (f32[2,1,2,128,128]{4,3,2,1,0:T(8,128)}, f32[2,1,2,128,128]{4,3,2,1,0:T(8,128)S(1)}, u32[]{:S(2)}, u32[]{:S(2)}) collective-permute-start(f32[2,1,2,128,128]{4,3,2,1,0:T(8,128)} %own_ref.1), channel_id=1, source_target_pairs={{0,4},{4,0},{8,12},{12,8},{16,20},{20,16},{24,28},{28,24},{1,2},{5... | collective-permute-start | bytes 786440 | tf_op jit(solution)/shard_map/ppermute | solution.py:116
  8.4 1.4 %copy-start = (f32[4,1,3,2,128,128]{5,4,3,2,1,0:T(8,128)S(1)}, f32[4,1,3,2,128,128]{5,4,3,2,1,0:T(8,128)}, u32[]{:S(2)}) copy-start(f32[4,1,3,2,128,128]{5,4,3,2,1,0:T(8,128)} %couple_ref.1) | copy-start | bytes 4718596
  9.8 0.9 %copy-start.1 = (f32[2,1,2,128,128]{4,3,2,1,0:T(8,128)S(1)}, f32[2,1,2,128,128]{4,3,2,1,0:T(8,128)}, u32[]{:S(2)}) copy-start(f32[2,1,2,128,128]{4,3,2,1,0:T(8,128)} %own_ref.1) | copy-start | bytes 786436
  10.7 0.7 %copy-start.3 = (s32[4]{0:T(128)S(1)}, s32[4]{0:T(128)}, u32[]{:S(2)}) copy-start(s32[4]{0:T(128)} %shifts_ref.1) | copy-start | bytes 52
  11.4 0.7 %copy-start.4 = (f32[4]{0:T(128)S(1)}, f32[4]{0:T(128)}, u32[]{:S(2)}) copy-start(f32[4]{0:T(128)} %occupation_ref.1) | copy-start | bytes 52
  12.0 0.7 %copy-start.5 = (s32[1,3]{1,0:T(1,128)S(1)}, s32[1,3]{1,0:T(1,128)}, u32[]{:S(2)}) copy-start(s32[1,3]{1,0:T(1,128)} %neighbours_ref.1) | copy-start | bytes 40
  16.6 0.7 %copy-start.2 = (f32[2,1,2,128,128]{4,3,2,1,0:T(8,128)}, f32[2,1,2,128,128]{4,3,2,1,0:T(8,128)S(1)}, u32[]{:S(2)}) copy-start(f32[2,1,2,128,128]{4,3,2,1,0:T(8,128)S(1)} %get-tuple-element.8.stay_ref) | copy-start | bytes 786436
  17.3 3.0 %collective-permute-start.2 = (f32[2,1,2,128,128]{4,3,2,1,0:T(8,128)S(1)}, f32[2,1,2,128,128]{4,3,2,1,0:T(8,128)S(1)}, u32[]{:S(2)}, u32[]{:S(2)}) collective-permute-start(f32[2,1,2,128,128]{4,3,2,1,0:T(8,128)S(1)} %get-tuple-element.9), channel_id=1, source_target_pairs={{0,4},{1,5},{2,6},{3,7},{4,0},{5,1},{6,2},{7,3},{8,12},{9,13},{10,... | collective-permute-start | bytes 786440 | tf_op jit(solution)/shard_map/ppermute | solution.py:116
  19.2 8.9 %collective-permute-start.3 = (f32[2,1,2,128,128]{4,3,2,1,0:T(8,128)S(1)}, f32[2,1,2,128,128]{4,3,2,1,0:T(8,128)S(1)}, u32[]{:S(2)}, u32[]{:S(2)}) collective-permute-start(f32[2,1,2,128,128]{4,3,2,1,0:T(8,128)S(1)} %get-tuple-element.10), channel_id=1, source_target_pairs={{0,1},{1,0},{2,3},{3,2},{4,8},{5,9},{6,10},{7,11},{8,4},{9,5},{10,... | collective-permute-start | bytes 786440 | tf_op jit(solution)/shard_map/ppermute | solution.py:116
  20.3 7.7 %copy-start.6 = (f32[2,1,2,128,128]{4,3,2,1,0:T(8,128)}, f32[2,1,2,128,128]{4,3,2,1,0:T(8,128)S(1)}, u32[]{:S(2)}) copy-start(f32[2,1,2,128,128]{4,3,2,1,0:T(8,128)S(1)} %collective-permute-done.2.got_even_ref) | copy-start | bytes 786436
  28.0 0.7 %copy-start.7 = (f32[2,1,2,128,128]{4,3,2,1,0:T(8,128)}, f32[2,1,2,128,128]{4,3,2,1,0:T(8,128)S(1)}, u32[]{:S(2)}) copy-start(f32[2,1,2,128,128]{4,3,2,1,0:T(8,128)S(1)} %collective-permute-done.3.got_odd_ref) | copy-start | bytes 786436

commit v2 on v1

v2 whole, which is shorter than its diff:
```python
import functools

import jax
import jax.numpy as jnp
from jax import lax
from jax.experimental import pallas as pl
from jax.experimental.pallas import tpu as pltpu
from jax.sharding import PartitionSpec as P

BYTES = 1 << 20


def neighbour_pairs(mesh, axis, other, odd):
    count, count_other = mesh.shape[axis], mesh.shape[other]
    axes = tuple(mesh.axis_names)
    pairs = []
    for here in range(count):
        there = here ^ 1 if not odd else ((here + 1) ^ 1) - 1
        for side in range(count_other):
            inside = 0 <= there < count
            source = {axis: here, other: side}
            target = {axis: there, other: side} if inside else {axis: here, other: side ^ 1}
            if target[other] < count_other:
                flat = [at[axes[0]] * mesh.shape[axes[1]] + at[axes[1]] for at in (source, target)]
                pairs.append((flat[0], flat[1]))
    return axes, pairs


def split(value):
    high = value.astype(jnp.bfloat16)
    return high, (value - high.astype(jnp.float32)).astype(jnp.bfloat16)


def product(lead_high, lead_low, trail_high, trail_low, contract):
    dims = (((1,), (contract,)), ((), ()))
    dot = functools.partial(lax.dot_general, dimension_numbers=dims, preferred_element_type=jnp.float32)
    return dot(lead_high, trail_high) + (dot(lead_low, trail_high) + dot(lead_high, trail_low))


def embed(target, index, real, imag, size):
    for part, (real_part, imag_part) in enumerate(zip(split(real), split(imag))):
        target[*index, part, :size, :size] = real_part
        target[*index, part, :size, size:] = imag_part
        target[*index, part, size:, :size] = -imag_part
        target[*index, part, size:, size:] = real_part


def prepare_kernel(own_ref, couple_ref, own_embed, lead, back):
    energies, _, _, size, _ = own_ref.shape
    modes, _, blocks = couple_ref.shape[:3]
    for energy in range(energies):
        embed(own_embed, (energy,), own_ref[energy, 0, 0], own_ref[energy, 0, 1], size)
    for block in range(blocks):
        for mode in range(modes):
            real, imag = couple_ref[mode, 0, block, 0], couple_ref[mode, 0, block, 1]
            rows = slice(mode * size, (mode + 1) * size)
            for part, (real_part, imag_part) in enumerate(zip(split(real), split(imag))):
                lead[block, part, rows, :size] = real_part
                lead[block, part, rows, size:] = imag_part
            embed(back, (mode, block), real, imag, size)


def energy_at(step, energies):
    return jnp.where(lax.rem(lax.axis_index("energy"), 2) == 0, step, energies - 1 - step)


def sandwich_kernel(
    step, shifts_hbm, occupation_hbm, neighbours_hbm, own_embed, even_ref, odd_ref, lead, back, *rest,
):
    energies, _, _, size, _ = even_ref.shape
    blocks, _, _, _ = lead.shape
    modes = back.shape[0]
    last = step == energies - 1
    if step:
        before, *rest = rest
    if last:
        stay_ref, give_even_ref, give_odd_ref, *rest = rest
    else:
        after, give_odd_ref, *rest = rest
    got_embed, shifts, occupation, neighbours, sems = rest[:5]
    total = rest[5] if last else after
    scalars = [
        pltpu.make_async_copy(source, target, sems.at[index])
        for index, (source, target) in enumerate(
            ((neighbours_hbm, neighbours), (shifts_hbm, shifts), (occupation_hbm, occupation))
        )
    ]
    for copy in scalars:
        copy.start()
    even_place = lax.rem(lax.axis_index("energy"), 2) == 0
    energy = energy_at(step, energies)
    got_embed[0] = own_embed[energy]
    for source, ref in enumerate((even_ref, odd_ref)):
        embed(got_embed, (source + 1,), ref[energy, 0, 0], ref[energy, 0, 1], size)
    if step:
        total[...] = before[...]
    else:
        total[...] = jnp.zeros_like(total)
    for copy in scalars:
        copy.wait()
    here = lax.axis_index("slab")
    ahead = 1 - 2 * lax.rem(here, 2)
    middles = []
    for block in range(blocks):
        offset = neighbours[0, block] - here
        source = jnp.where(offset == 0, 0, jnp.where(offset == ahead, 1, 2))
        middles.append(product(lead[block, 0], lead[block, 1], got_embed[source, 0], got_embed[source, 1], 0))
    for mode in range(modes):
        shift, number = shifts[mode], occupation[mode]
        rows = slice(mode * size, (mode + 1) * size)
        part = 0.0
        for block in range(blocks):
            high, low = split(middles[block][rows])
            part = part + product(high, low, back[mode, block, 0], back[mode, block, 1], 1)
        total[energy + energies - shift] += (number + 1.0) * part
        total[energy + energies + shift] += number * part

    def put(ref, row, slot):
        value = total[slot]
        ref[row, 0, 0] = value[:, :size]
        ref[row, 0, 1] = value[:, size:]

    put(give_odd_ref, 0, jnp.where(even_place, step, 3 * energies - 1 - step))
    if last:
        for row in range(energies):
            put(stay_ref, row, energies + row)
            put(give_even_ref, row, jnp.where(even_place, 2 * energies, 0) + row)


def sum_kernel(ends, stay_ref, got_even_ref, *rest):
    got_odd_refs, out_ref = rest[:-1], rest[-1]
    energies = stay_ref.shape[0]
    place = lax.axis_index("energy")
    inside = jnp.logical_and(place != 0, place != ends)
    out_ref[...] = stay_ref[...] + got_even_ref[...]
    for step, ref in enumerate(got_odd_refs):
        row = jnp.where(lax.rem(place, 2) == 0, energies - 1 - step, step)
        out_ref[row] += jnp.where(inside, ref[0], 0.0)


def shards(mesh, green_lesser, coupling, occupation, shifts, neighbours):
    energies, _, _, size, _ = green_lesser.shape
    modes, _, blocks = coupling.shape[:3]
    swap = lambda value, axis, other, odd: lax.ppermute(value, *neighbour_pairs(mesh, axis, other, odd))
    vmem = pl.BlockSpec(memory_space=pltpu.VMEM)
    hbm = pl.BlockSpec(memory_space=pl.ANY)
    whole = lambda array: pl.BlockSpec(array.shape, lambda: (0,) * array.ndim)
    params = lambda mib: pltpu.CompilerParams(vmem_limit_bytes=mib * BYTES)
    half = lambda *shape: jax.ShapeDtypeStruct(shape, jnp.bfloat16)
    full = lambda *shape: jax.ShapeDtypeStruct(shape, jnp.float32)

    even = swap(green_lesser, "slab", "energy", False)
    odd = swap(green_lesser, "slab", "energy", True)
    own_embed, lead, back = pl.pallas_call(
        prepare_kernel,
        out_shape=[
            half(energies, 2, 2 * size, 2 * size),
            half(blocks, 2, modes * size, 2 * size),
            half(modes, blocks, 2, 2 * size, 2 * size),
        ],
        in_specs=[whole(green_lesser), whole(coupling)],
        out_specs=[vmem] * 3,
        compiler_params=params(8),
        cost_estimate=pl.CostEstimate(flops=0, bytes_accessed=8 * BYTES, transcendentals=0),
    )(green_lesser, coupling)
    totals = (3 * energies, size, 2 * size)
    got_odds = []
    before = []
    for step in range(energies):
        last = step == energies - 1
        give = full(1, *green_lesser.shape[1:])
        results = pl.pallas_call(
            functools.partial(sandwich_kernel, step),
            out_shape=[full(*green_lesser.shape)] * 2 + [give] if last else [full(*totals), give],
            in_specs=[hbm] * 3 + [vmem] * (5 + len(before)),
            out_specs=[vmem] * (3 if last else 2),
            scratch_shapes=[
                pltpu.VMEM((3, 2, 2 * size, 2 * size), jnp.bfloat16),
                pltpu.SMEM(shifts.shape, jnp.int32),
                pltpu.SMEM(occupation.shape, jnp.float32),
                pltpu.SMEM(neighbours.shape, jnp.int32),
                pltpu.SemaphoreType.DMA((3,)),
            ]
            + ([pltpu.VMEM(totals, jnp.float32)] if last else []),
            compiler_params=params(8),
            cost_estimate=pl.CostEstimate(flops=2 * 10**9, bytes_accessed=8 * BYTES, transcendentals=0),
        )(shifts, occupation, neighbours, own_embed, even, odd, lead, back, *before)
        got_odds.append(swap(results[-1], "energy", "slab", True))
        before = [results[0]]
    stay, give_even, _ = results
    got_even = swap(give_even, "energy", "slab", False)
    return pl.pallas_call(
        functools.partial(sum_kernel, mesh.shape["energy"] - 1),
        out_shape=full(*green_lesser.shape),
        in_specs=[vmem] * (2 + energies),
        out_specs=whole(green_lesser),
        compiler_params=params(4),
    )(stay, got_even, *got_odds)


def solution(mesh):
    placed = (
        P("energy", "slab", None, None, None),
        P(None, "slab", None, None, None, None),
        P(),
        P(),
        P("slab", None),
    )
    return jax.shard_map(
        functools.partial(shards, mesh),
        mesh=mesh,
        in_specs=placed,
        out_specs=P("energy", "slab", None, None, None),
        check_vma=False,
    )
```

time: 30.8 us -> 26.1 us (0.85)
  the two profiles are of different devices: /device:TPU:19 before, /device:TPU:1 now
where the time goes in v2:
time: 26.1 us; the launch traced here: 25.9 us
  waiting for transfers between devices  9.41 us (36%)
  Pallas kernels  7.29 us (28%)
  starting transfers between devices  6.77 us (26%)
  local copies, waits for them, and re-layouts  2.37 us (9%)
    ppermute x5, waiting for transfers between devices, shards(): lax.ppermute(value, *neighbour_pairs(mesh, axis, other, odd))  9.41 us
    ppermute x5, starting transfers between devices, shards(): lax.ppermute(value, *neighbour_pairs(mesh, axis, other, odd))  6.77 us
    pallas_call x2, Pallas kernels, shards(): pl.pallas_call(functools.partial(sandwich_kernel, step), out_shape=[full(...  5.83 us
    unnamed x10, local copies, waits for them, and re-layouts  2.37 us
    pallas_call x1, Pallas kernels, shards(): pl.pallas_call(functools.partial(sum_kernel, mesh.shape['energy'] - 1), o...  0.78 us
    pallas_call x1, Pallas kernels, shards(): pl.pallas_call(prepare_kernel, out_shape=[half(energies, 2, 2 * size, 2 *...  0.68 us
  transfers between devices with their start and end apart: 5, of which 3 were waited for; matrix products, arithmetic and copies ran while one was open for 0% of the time, Pallas kernels for 3%

profile of v2, /device:TPU:1, one launch (start us, length us, event | category | flops | bytes accessed | tf_op | source)
XLA Modules:
  0.0 25.9 jit_solution(14600674569031938093)
XLA Ops:
  0.0 0.1 collective-permute-start.1
  0.1 3.4 %collective-permute-start = (f32[2,1,2,128,128]{4,3,2,1,0:T(8,128)}, f32[2,1,2,128,128]{4,3,2,1,0:T(8,128)S(1)}, u32[]{:S(2)}, u32[]{:S(2)}) collective-permute-start(f32[2,1,2,128,128]{4,3,2,1,0:T(8,128)} %own_ref.1), channel_id=1, source_target_pairs={{0,1},{4,5},{8,9},{12,13},{16,17},{20,21},{24,25},{28,29},{1,0},{5... | collective-permute-start | bytes 786440 | tf_op jit(solution)/shard_map/ppermute | solution.py:144
  3.4 0.0 copy-start
  3.4 1.4 %copy-done = f32[4,1,3,2,128,128]{5,4,3,2,1,0:T(8,128)S(1)} copy-done((f32[4,1,3,2,128,128]{5,4,3,2,1,0:T(8,128)S(1)}, f32[4,1,3,2,128,128]{5,4,3,2,1,0:T(8,128)}, u32[]{:S(2)}) %copy-start) | copy-done | bytes 1572888
  4.8 0.0 copy-start.1
  4.8 0.9 %copy-done.1 = f32[2,1,2,128,128]{4,3,2,1,0:T(8,128)S(1)} copy-done((f32[2,1,2,128,128]{4,3,2,1,0:T(8,128)S(1)}, f32[2,1,2,128,128]{4,3,2,1,0:T(8,128)}, u32[]{:S(2)}) %copy-start.1) | copy-done | bytes 262168
  5.8 0.0 copy-start.2
  5.8 0.0 copy-start.3
  5.8 0.0 copy-start.4
  5.8 0.7 %shard_map.55 = (bf16[2,2,256,256]{3,2,1,0:T(8,128)(2,1)S(1)}, bf16[3,2,512,256]{3,2,1,0:T(8,128)(2,1)S(1)}, bf16[4,3,2,256,256]{4,3,2,1,0:T(8,128)(2,1)S(1)}) custom-call(f32[2,1,2,128,128]{4,3,2,1,0:T(8,128)S(1)} %copy-done.1, f32[4,1,3,2,128,128]{5,4,3,2,1,0:T(8,128)S(1)} %copy-done), custom_call_target="tpu_custom_call" | custom-call | bytes 8388608 | tf_op jit(solution)/shard_map/pallas_call | solution.py:154
  6.5 0.0 collective-permute-done.1.odd_ref
  6.5 2.9 %collective-permute-done.even_ref = f32[2,1,2,128,128]{4,3,2,1,0:T(8,128)S(1)} collective-permute-done((f32[2,1,2,128,128]{4,3,2,1,0:T(8,128)}, f32[2,1,2,128,128]{4,3,2,1,0:T(8,128)S(1)}, u32[]{:S(2)}, u32[]{:S(2)}) %collective-permute-start) | collective-permute-done | bytes 262176 | tf_op jit(solution)/shard_map/ppermute | solution.py:144
  9.4 0.0 copy-done.2
  9.4 0.0 copy-done.3
  9.4 0.0 copy-done.4
  9.4 2.9 %shard_map.56 = (f32[6,128,256]{2,1,0:T(8,128)S(1)}, f32[1,1,2,128,128]{4,3,2,1,0:T(8,128)S(1)}) custom-call(s32[4]{0:T(128)S(1)} %copy-done.2, f32[4]{0:T(128)S(1)} %copy-done.3, s32[1,3]{1,0:T(1,128)S(1)} %copy-done.4, bf16[2,2,256,256]{3,2,1,0:T(8,128)(2,1)S(1)} %get-tuple-element.13.own_embed, f32[2,1,2,128,128]{4,3,2,1,0:T(8,128)S(1)} %collective-permute-done.even_ref, ...), custom_call_target="tpu_custom_call" | custom-call | flops 2000000000 | bytes 8388608 | tf_op jit(solution)/shard_map/pallas_call | solution.py:172
  12.3 2.9 %shard_map.57 = (f32[2,1,2,128,128]{4,3,2,1,0:T(8,128)S(1)}, f32[2,1,2,128,128]{4,3,2,1,0:T(8,128)S(1)}, f32[1,1,2,128,128]{4,3,2,1,0:T(8,128)S(1)}) custom-call(s32[4]{0:T(128)S(1)} %copy-done.2, f32[4]{0:T(128)S(1)} %copy-done.3, s32[1,3]{1,0:T(1,128)S(1)} %copy-done.4, bf16[2,2,256,256]{3,2,1,0:T(8,128)(2,1)S(1)} %get-tuple-element.13.own_embed, ...), custom_call_target="tpu_custom_call" | custom-call | flops 2000000000 | bytes 8388608 | tf_op jit(solution)/shard_map/pallas_call | solution.py:172
  15.2 1.6 %collective-permute-start.2 = (f32[2,1,2,128,128]{4,3,2,1,0:T(8,128)S(1)}, f32[2,1,2,128,128]{4,3,2,1,0:T(8,128)S(1)}, u32[]{:S(2)}, u32[]{:S(2)}) collective-permute-start(f32[2,1,2,128,128]{4,3,2,1,0:T(8,128)S(1)} %get-tuple-element.18), channel_id=1, source_target_pairs={{0,4},{1,5},{2,6},{3,7},{4,0},{5,1},{6,2},{7,3},{8,12},{9,13},{10,... | collective-permute-start | bytes 786440 | tf_op jit(solution)/shard_map/ppermute | solution.py:144
  16.8 1.2 %collective-permute-start.4 = (f32[1,1,2,128,128]{4,3,2,1,0:T(8,128)S(1)}, f32[1,1,2,128,128]{4,3,2,1,0:T(8,128)S(1)}, u32[]{:S(2)}, u32[]{:S(2)}) collective-permute-start(f32[1,1,2,128,128]{4,3,2,1,0:T(8,128)S(1)} %get-tuple-element.20), channel_id=1, source_target_pairs={{0,1},{1,0},{2,3},{3,2},{4,8},{5,9},{6,10},{7,11},{8,4},{9,5},{10,... | collective-permute-start | bytes 393224 | tf_op jit(solution)/shard_map/ppermute | solution.py:144
  18.0 0.6 %collective-permute-start.3 = (f32[1,1,2,128,128]{4,3,2,1,0:T(8,128)S(1)}, f32[1,1,2,128,128]{4,3,2,1,0:T(8,128)S(1)}, u32[]{:S(2)}, u32[]{:S(2)}) collective-permute-start(f32[1,1,2,128,128]{4,3,2,1,0:T(8,128)S(1)} %get-tuple-element.19), channel_id=1, source_target_pairs={{0,1},{1,0},{2,3},{3,2},{4,8},{5,9},{6,10},{7,11},{8,4},{9,5},{10,... | collective-permute-start | bytes 393224 | tf_op jit(solution)/shard_map/ppermute | solution.py:144
  18.6 4.0 %collective-permute-done.4.rest_1_ = f32[1,1,2,128,128]{4,3,2,1,0:T(8,128)S(1)} collective-permute-done((f32[1,1,2,128,128]{4,3,2,1,0:T(8,128)S(1)}, f32[1,1,2,128,128]{4,3,2,1,0:T(8,128)S(1)}, u32[]{:S(2)}, u32[]{:S(2)}) %collective-permute-start.4) | collective-permute-done | bytes 131104 | tf_op jit(solution)/shard_map/ppermute | solution.py:144
  22.6 2.5 %collective-permute-done.3.rest_0_ = f32[1,1,2,128,128]{4,3,2,1,0:T(8,128)S(1)} collective-permute-done((f32[1,1,2,128,128]{4,3,2,1,0:T(8,128)S(1)}, f32[1,1,2,128,128]{4,3,2,1,0:T(8,128)S(1)}, u32[]{:S(2)}, u32[]{:S(2)}) %collective-permute-start.3) | collective-permute-done | bytes 131104 | tf_op jit(solution)/shard_map/ppermute | solution.py:144
  25.1 0.0 collective-permute-done.2.got_even_ref
  25.1 0.8 %shard_map.58 = f32[2,1,2,128,128]{4,3,2,1,0:T(8,128)} custom-call(f32[2,1,2,128,128]{4,3,2,1,0:T(8,128)S(1)} %get-tuple-element.17.stay_ref, f32[2,1,2,128,128]{4,3,2,1,0:T(8,128)S(1)} %collective-permute-done.2.got_even_ref, f32[1,1,2,128,128]{4,3,2,1,0:T(8,128)S(1)} %collective-permute-done.3.rest_0_, ...), custom_call_target="tpu_custom_call" | custom-call | tf_op jit(solution)/shard_map/pallas_call | solution.py:192
Async XLA Ops:
  0.0 6.5 %collective-permute-start.1 = (f32[2,1,2,128,128]{4,3,2,1,0:T(8,128)}, f32[2,1,2,128,128]{4,3,2,1,0:T(8,128)S(1)}, u32[]{:S(2)}, u32[]{:S(2)}) collective-permute-start(f32[2,1,2,128,128]{4,3,2,1,0:T(8,128)} %own_ref.1), channel_id=1, source_target_pairs={{0,4},{4,0},{8,12},{12,8},{16,20},{20,16},{24,28},{28,24},{1,2},{5... | collective-permute-start | bytes 786440 | tf_op jit(solution)/shard_map/ppermute | solution.py:144
  0.1 9.3 %collective-permute-start = (f32[2,1,2,128,128]{4,3,2,1,0:T(8,128)}, f32[2,1,2,128,128]{4,3,2,1,0:T(8,128)S(1)}, u32[]{:S(2)}, u32[]{:S(2)}) collective-permute-start(f32[2,1,2,128,128]{4,3,2,1,0:T(8,128)} %own_ref.1), channel_id=1, source_target_pairs={{0,1},{4,5},{8,9},{12,13},{16,17},{20,21},{24,25},{28,29},{1,0},{5... | collective-permute-start | bytes 786440 | tf_op jit(solution)/shard_map/ppermute | solution.py:144
  3.4 1.4 %copy-start = (f32[4,1,3,2,128,128]{5,4,3,2,1,0:T(8,128)S(1)}, f32[4,1,3,2,128,128]{5,4,3,2,1,0:T(8,128)}, u32[]{:S(2)}) copy-start(f32[4,1,3,2,128,128]{5,4,3,2,1,0:T(8,128)} %couple_ref.1) | copy-start | bytes 4718596
  4.8 0.9 %copy-start.1 = (f32[2,1,2,128,128]{4,3,2,1,0:T(8,128)S(1)}, f32[2,1,2,128,128]{4,3,2,1,0:T(8,128)}, u32[]{:S(2)}) copy-start(f32[2,1,2,128,128]{4,3,2,1,0:T(8,128)} %own_ref.1) | copy-start | bytes 786436
  5.8 3.6 %copy-start.2 = (s32[4]{0:T(128)S(1)}, s32[4]{0:T(128)}, u32[]{:S(2)}) copy-start(s32[4]{0:T(128)} %shifts_hbm.3) | copy-start | bytes 52
  5.8 3.6 %copy-start.3 = (f32[4]{0:T(128)S(1)}, f32[4]{0:T(128)}, u32[]{:S(2)}) copy-start(f32[4]{0:T(128)} %occupation_hbm.3) | copy-start | bytes 52
  5.8 3.6 %copy-start.4 = (s32[1,3]{1,0:T(1,128)S(1)}, s32[1,3]{1,0:T(1,128)}, u32[]{:S(2)}) copy-start(s32[1,3]{1,0:T(1,128)} %neighbours_hbm.3) | copy-start | bytes 40
  15.2 9.9 %collective-permute-start.2 = (f32[2,1,2,128,128]{4,3,2,1,0:T(8,128)S(1)}, f32[2,1,2,128,128]{4,3,2,1,0:T(8,128)S(1)}, u32[]{:S(2)}, u32[]{:S(2)}) collective-permute-start(f32[2,1,2,128,128]{4,3,2,1,0:T(8,128)S(1)} %get-tuple-element.18), channel_id=1, source_target_pairs={{0,4},{1,5},{2,6},{3,7},{4,0},{5,1},{6,2},{7,3},{8,12},{9,13},{10,... | collective-permute-start | bytes 786440 | tf_op jit(solution)/shard_map/ppermute | solution.py:144
  16.8 5.7 %collective-permute-start.4 = (f32[1,1,2,128,128]{4,3,2,1,0:T(8,128)S(1)}, f32[1,1,2,128,128]{4,3,2,1,0:T(8,128)S(1)}, u32[]{:S(2)}, u32[]{:S(2)}) collective-permute-start(f32[1,1,2,128,128]{4,3,2,1,0:T(8,128)S(1)} %get-tuple-element.20), channel_id=1, source_target_pairs={{0,1},{1,0},{2,3},{3,2},{4,8},{5,9},{6,10},{7,11},{8,4},{9,5},{10,... | collective-permute-start | bytes 393224 | tf_op jit(solution)/shard_map/ppermute | solution.py:144
  18.0 7.1 %collective-permute-start.3 = (f32[1,1,2,128,128]{4,3,2,1,0:T(8,128)S(1)}, f32[1,1,2,128,128]{4,3,2,1,0:T(8,128)S(1)}, u32[]{:S(2)}, u32[]{:S(2)}) collective-permute-start(f32[1,1,2,128,128]{4,3,2,1,0:T(8,128)S(1)} %get-tuple-element.19), channel_id=1, source_target_pairs={{0,1},{1,0},{2,3},{3,2},{4,8},{5,9},{6,10},{7,11},{8,4},{9,5},{10,... | collective-permute-start | bytes 393224 | tf_op jit(solution)/shard_map/ppermute | solution.py:144

commit v3 on v0

v3 whole, which is shorter than its diff:
```python
import functools

import jax
import jax.numpy as jnp
from jax import lax
from jax.experimental import pallas as pl
from jax.experimental.pallas import tpu as pltpu
from jax.sharding import PartitionSpec as P

BYTES = 1 << 20
ROWS = 8


def neighbour_pairs(mesh, axis, other, odd):
    count, count_other = mesh.shape[axis], mesh.shape[other]
    axes = tuple(mesh.axis_names)
    pairs = []
    for here in range(count):
        there = here ^ 1 if not odd else ((here + 1) ^ 1) - 1
        for side in range(count_other):
            inside = 0 <= there < count
            source = {axis: here, other: side}
            target = {axis: there, other: side} if inside else {axis: here, other: side ^ 1}
            if target[other] < count_other:
                flat = [at[axes[0]] * mesh.shape[axes[1]] + at[axes[1]] for at in (source, target)]
                pairs.append((flat[0], flat[1]))
    return axes, pairs


def even_place():
    return lax.rem(lax.axis_index("energy"), 2) == 0


def row_of(number, energies):
    return jnp.where(even_place(), number, energies - 1 - number)


def split(value):
    high = value.astype(jnp.bfloat16)
    return high, (value - high.astype(jnp.float32)).astype(jnp.bfloat16)


def product(lead_high, lead_low, trail_high, trail_low):
    dot = functools.partial(jnp.dot, preferred_element_type=jnp.float32)
    return dot(lead_high, trail_high) + (dot(lead_low, trail_high) + dot(lead_high, trail_low))


def embed(target, index, real, imag, size):
    for part, (real_part, imag_part) in enumerate(zip(split(real), split(imag))):
        target[*index, part, :size, :size] = real_part
        target[*index, part, :size, size:] = imag_part
        target[*index, part, size:, :size] = -imag_part
        target[*index, part, size:, size:] = real_part


def near_kernel(own_ref, near_ref, sem):
    copy = pltpu.make_async_copy(own_ref.at[pl.ds(row_of(0, own_ref.shape[0]), 1)], near_ref, sem)
    copy.start()
    copy.wait()


def prepare_kernel(
    ends, energies, shifts_hbm, occupation_hbm, neighbours_hbm, couple_ref,
    lead, back, is_own, is_even, down, up, foreign_up, shifts, occupation, neighbours, sems,
):
    modes, _, blocks, _, size, _ = couple_ref.shape
    copies = [
        pltpu.make_async_copy(source, target, sems.at[index])
        for index, (source, target) in enumerate(
            ((shifts_hbm, shifts), (occupation_hbm, occupation), (neighbours_hbm, neighbours))
        )
    ]
    for copy in copies:
        copy.start()
    for mode in range(modes):
        for block in range(blocks):
            real, imag = couple_ref[mode, 0, block, 0], couple_ref[mode, 0, block, 1]
            rows = slice(mode * size, (mode + 1) * size)
            for part, (real_part, imag_part) in enumerate(zip(split(real), split(imag))):
                lead[block, part, rows, :size] = real_part
                lead[block, part, rows, size:] = imag_part
            embed(back, (mode, block), real.T, -imag.T, size)
    for copy in copies:
        copy.wait()
    here, place = lax.axis_index("slab"), lax.axis_index("energy")
    ahead = 1 - 2 * lax.rem(here, 2)
    wide = (ROWS, 2 * size)
    for block in range(blocks):
        offset = neighbours[0, block] - here
        is_own[block] = jnp.full(wide, jnp.where(offset == 0, 1.0, 0.0), jnp.float32)
        is_even[block] = jnp.full(wide, jnp.where(offset == ahead, 1.0, 0.0), jnp.float32)
    inside = jnp.logical_and(place != 0, place != ends)
    for mode in range(modes):
        less, more = occupation[mode], occupation[mode] + 1.0
        down_weight = jnp.where(even_place(), more, less)
        up_weight = jnp.where(even_place(), less, more)
        for shift in range(1, energies + 1):
            chosen = shifts[mode] == shift
            for ref, weight in (
                (down, down_weight), (up, up_weight), (foreign_up, jnp.where(inside, up_weight, 0.0)),
            ):
                ref[mode, shift - 1] = jnp.full(wide, jnp.where(chosen, weight, 0.0), jnp.float32)


def scaled(value, weight):
    return (value.reshape(-1, ROWS, value.shape[1]) * weight[None]).reshape(value.shape)


def sandwiches(own, even, odd, is_own, is_even, lead, back, embeds):
    blocks, size = lead.shape[0], lead.shape[3] // 2
    middles = []
    for block in range(blocks):
        take_own = is_own[block][None, :, :size] != 0.0
        take_even = is_even[block][None, :, :size] != 0.0
        tiles = (size // ROWS, ROWS, size)
        parts = [
            jnp.where(
                take_own, own(part).reshape(tiles),
                jnp.where(take_even, even(part).reshape(tiles), odd(part).reshape(tiles)),
            ).reshape(size, size)
            for part in range(2)
        ]
        embed(embeds, (block,), *parts, size)
        middles.append(product(lead[block, 0], lead[block, 1], embeds[block, 0], embeds[block, 1]))
    for mode in range(back.shape[0]):
        rows = slice(mode * size, (mode + 1) * size)
        total = 0.0
        for block in range(blocks):
            high, low = split(middles[block][rows])
            total = total + product(high, low, back[mode, block, 0], back[mode, block, 1])
        yield mode, total


def put(ref, row, value, add=None):
    size = value.shape[0]
    for part in range(2):
        one = value[:, part * size : (part + 1) * size]
        ref[row, 0, part] = one if add is None else add[row, 0, part] + one


def far_kernel(
    own_ref, even_ref, odd_ref, is_own, is_even, down, up, lead, back, give_ref, stay_ref, give_more_ref, embeds
):
    energies, _, _, size, _ = own_ref.shape
    totals = {}
    for number in range(1, energies):
        row = row_of(number, energies)
        reader = lambda ref: lambda part: ref[row, 0, part]
        for mode, value in sandwiches(
            reader(own_ref), reader(even_ref), reader(odd_ref), is_own, is_even, lead, back, embeds
        ):
            for shift in range(1, energies + 1):
                for target, weights in ((number - shift, down), (number + shift, up)):
                    if -energies < target < 2 * energies:
                        totals[target] = totals.get(target, 0.0) + scaled(value, weights[mode, shift - 1])
    zero = jnp.zeros((size, 2 * size), jnp.float32)
    for index in range(energies - 1):
        put(give_ref, index, totals.get(-1 - index, zero))
    for index in range(energies):
        put(stay_ref, index, totals.get(index, zero))
        put(give_more_ref, index, totals.get(energies + index, zero))


def near_far_kernel(
    own_ref, even_ref, odd_ref, is_own, is_even, up, lead, back, stay_before, give_before, stay_ref, give_ref, embeds
):
    energies, _, _, size, _ = own_ref.shape
    row = row_of(0, energies)
    reader = lambda ref: lambda part: ref[row, 0, part]
    totals = {}
    for mode, value in sandwiches(
        reader(own_ref), reader(even_ref), reader(odd_ref), is_own, is_even, lead, back, embeds
    ):
        for shift in range(1, energies + 1):
            totals[shift] = totals.get(shift, 0.0) + scaled(value, up[mode, shift - 1])
    for index in range(energies):
        if index in totals:
            put(stay_ref, index, totals[index], stay_before)
        else:
            stay_ref[index] = stay_before[index]
        if energies + index in totals:
            put(give_ref, index, totals[energies + index], give_before)
        else:
            give_ref[index] = give_before[index]


def foreign_kernel(own_ref, even_ref, odd_ref, is_own, is_even, up, lead, back, before, stay_ref, embeds):
    energies = before.shape[0]
    reader = lambda ref: lambda part: ref[0, 0, part]
    totals = {}
    for mode, value in sandwiches(
        reader(own_ref), reader(even_ref), reader(odd_ref), is_own, is_even, lead, back, embeds
    ):
        for shift in range(1, energies + 1):
            totals[shift] = totals.get(shift, 0.0) + scaled(value, up[mode, shift - 1])
    for index in range(energies):
        put(stay_ref, index, totals[index + 1], before)


def border_kernel(ends, before, got_odd_ref, stay_ref):
    place = lax.axis_index("energy")
    inside = jnp.logical_and(place != 0, place != ends)
    energies = before.shape[0]
    for number in range(energies - 1):
        stay_ref[number] = before[number] + jnp.where(inside, got_odd_ref[number], 0.0)
    stay_ref[energies - 1] = before[energies - 1]


def sum_kernel(stay_ref, got_even_ref, out_ref):
    energies = stay_ref.shape[0]
    for number in range(energies):
        out_ref[row_of(number, energies)] = stay_ref[number] + got_even_ref[energies - 1 - number]


def shards(mesh, green_lesser, coupling, occupation, shifts, neighbours):
    energies, _, _, size, _ = green_lesser.shape
    modes, _, blocks = coupling.shape[:3]
    ends = mesh.shape["energy"] - 1
    swap = lambda value, axis, other, odd: lax.ppermute(value, *neighbour_pairs(mesh, axis, other, odd))
    slabs = lambda value: [swap(value, "slab", "energy", odd) for odd in (False, True)]
    vmem = pl.BlockSpec(memory_space=pltpu.VMEM)
    hbm = pl.BlockSpec(memory_space=pltpu.HBM)
    half = lambda *shape: jax.ShapeDtypeStruct(shape, jnp.bfloat16)
    full = lambda *shape: jax.ShapeDtypeStruct(shape, jnp.float32)
    block = lambda count: full(count, *green_lesser.shape[1:])

    def call(kernel, outs, ins, args, mib, micros, **more):
        return pl.pallas_call(
            kernel,
            out_shape=outs,
            in_specs=ins,
            out_specs=more.pop("out_specs", [vmem] * len(outs)),
            compiler_params=pltpu.CompilerParams(vmem_limit_bytes=mib * BYTES),
            cost_estimate=pl.CostEstimate(flops=micros * 10**9, bytes_accessed=0, transcendentals=0),
            **more,
        )(*args)

    slab_own = slabs(green_lesser)
    (near,) = call(near_kernel, [block(1)], [hbm], [green_lesser], 2, 10, scratch_shapes=[pltpu.SemaphoreType.DMA])
    foreign = swap(near, "energy", "slab", True)
    slab_foreign = slabs(foreign)
    wide = (ROWS, 2 * size)
    lead, back, is_own, is_even, down, up, foreign_up = call(
        functools.partial(prepare_kernel, ends, energies),
        [half(blocks, 2, modes * size, 2 * size), half(modes, blocks, 2, 2 * size, 2 * size)]
        + [full(blocks, *wide)] * 2 + [full(modes, energies, *wide)] * 3,
        [hbm] * 3 + [vmem], [shifts, occupation, neighbours, coupling], 8, 2,
        scratch_shapes=[
            pltpu.SMEM(shifts.shape, jnp.int32),
            pltpu.SMEM(occupation.shape, jnp.float32),
            pltpu.SMEM(neighbours.shape, jnp.int32),
            pltpu.SemaphoreType.DMA((3,)),
        ],
    )
    embeds = [pltpu.VMEM((blocks, 2, 2 * size, 2 * size), jnp.bfloat16)]
    give_odd, stay, give_even = call(
        far_kernel, [block(energies - 1), block(energies), block(energies)], [vmem] * 9,
        [green_lesser, *slab_own, is_own, is_even, down, up, lead, back], 8, 10, scratch_shapes=embeds,
    )
    got_odd = swap(give_odd, "energy", "slab", True)
    stay, give_even = call(
        near_far_kernel, [block(energies)] * 2, [vmem] * 10,
        [green_lesser, *slab_own, is_own, is_even, up, lead, back, stay, give_even], 8, 10, scratch_shapes=embeds,
    )
    got_even = swap(give_even, "energy", "slab", False)
    (stay,) = call(
        foreign_kernel, [block(energies)], [vmem] * 9,
        [foreign, *slab_foreign, is_own, is_even, foreign_up, lead, back, stay], 8, 0, scratch_shapes=embeds,
    )
    (stay,) = call(
        functools.partial(border_kernel, ends), [block(energies)], [vmem] * 2, [stay, got_odd], 2, 10,
    )
    return call(
        sum_kernel, block(energies), [vmem] * 2, [stay, got_even], 4, 1,
        out_specs=pl.BlockSpec(green_lesser.shape, lambda: (0,) * green_lesser.ndim),
    )


def solution(mesh):
    placed = (
        P("energy", "slab", None, None, None),
        P(None, "slab", None, None, None, None),
        P(),
        P(),
        P("slab", None),
    )
    return jax.shard_map(
        functools.partial(shards, mesh),
        mesh=mesh,
        in_specs=placed,
        out_specs=P("energy", "slab", None, None, None),
        check_vma=False,
    )
```

time: 112 us -> 22.6 us (0.20)
  the two profiles are of different devices: /device:TPU:12 before, /device:TPU:1 now
where the time goes in v3:
time: 22.6 us; the launch traced here: 22.5 us
  starting transfers between devices  10.2 us (45%)
  Pallas kernels  7.73 us (34%)
  waiting for transfers between devices  3.48 us (15%)
  local copies, waits for them, and re-layouts  0.97 us (4%)
    ppermute x7, starting transfers between devices, shards(): lax.ppermute(value, *neighbour_pairs(mesh, axis, other, odd))  10.2 us
    pallas_call x7, Pallas kernels, call(): pl.pallas_call(kernel, out_shape=outs, in_specs=ins, out_specs=more.pop('...  7.73 us
    ppermute x7, waiting for transfers between devices, shards(): lax.ppermute(value, *neighbour_pairs(mesh, axis, other, odd))  3.48 us
    unnamed x12, local copies, waits for them, and re-layouts  0.97 us
  transfers between devices with their start and end apart: 7, of which 1 were waited for; matrix products, arithmetic and copies ran while one was open for 0% of the time, Pallas kernels for 31%

profile of v3, /device:TPU:1, one launch (start us, length us, event | category | flops | bytes accessed | tf_op | source)
XLA Modules:
  0.0 22.5 jit_solution(298189777052902225)
XLA Ops:
  0.0 2.1 %collective-permute-start.3 = (f32[2,1,2,128,128]{4,3,2,1,0:T(8,128)}, f32[2,1,2,128,128]{4,3,2,1,0:T(8,128)S(1)}, u32[]{:S(2)}, u32[]{:S(2)}) collective-permute-start(f32[2,1,2,128,128]{4,3,2,1,0:T(8,128)} %own_ref.5), channel_id=1, source_target_pairs={{0,1},{4,5},{8,9},{12,13},{16,17},{20,21},{24,25},{28,29},{1,0},{5... | collective-permute-start | bytes 786440 | tf_op jit(solution)/shard_map/ppermute | solution.py:219
  2.1 1.0 %collective-permute-start.4 = (f32[2,1,2,128,128]{4,3,2,1,0:T(8,128)}, f32[2,1,2,128,128]{4,3,2,1,0:T(8,128)S(1)}, u32[]{:S(2)}, u32[]{:S(2)}) collective-permute-start(f32[2,1,2,128,128]{4,3,2,1,0:T(8,128)} %own_ref.5), channel_id=1, source_target_pairs={{0,4},{4,0},{8,12},{12,8},{16,20},{20,16},{24,28},{28,24},{1,2},{5... | collective-permute-start | bytes 786440 | tf_op jit(solution)/shard_map/ppermute | solution.py:219
  3.1 0.9 %copy-done.1 = f32[2,1,2,128,128]{4,3,2,1,0:T(8,128)S(1)} copy-done((f32[2,1,2,128,128]{4,3,2,1,0:T(8,128)S(1)}, f32[2,1,2,128,128]{4,3,2,1,0:T(8,128)}, u32[]{:S(2)}) %copy-start.1) | copy-done | bytes 262168
  4.0 0.2 shard_map.55
  4.2 0.0 copy-start.2
  4.2 1.2 %collective-permute-start = (f32[1,1,2,128,128]{4,3,2,1,0:T(8,128)S(1)}, f32[1,1,2,128,128]{4,3,2,1,0:T(8,128)S(1)}, u32[]{:S(2)}, u32[]{:S(2)}) collective-permute-start(f32[1,1,2,128,128]{4,3,2,1,0:T(8,128)S(1)} %shard_map.55), channel_id=1, source_target_pairs={{0,1},{1,0},{2,3},{3,2},{4,8},{5,9},{6,10},{7,11},{8,4},{9,5},{10,... | collective-permute-start | bytes 393224 | tf_op jit(solution)/shard_map/ppermute | solution.py:219
  5.4 0.0 copy-done
  5.4 0.0 copy-done.4
  5.4 1.2 %shard_map.56 = (bf16[3,2,512,256]{3,2,1,0:T(8,128)(2,1)S(1)}, bf16[4,3,2,256,256]{4,3,2,1,0:T(8,128)(2,1)S(1)}, f32[3,8,256]{2,1,0:T(8,128)S(1)}, f32[3,8,256]{...) custom-call(s32[4]{0:T(128)S(1)} %copy-done.3, ...), custom_call_target="tpu_custom_call" | custom-call | flops 2000000000 | tf_op jit(solution)/shard_map/pallas_call | solution.py:228
  6.6 3.5 %collective-permute-done.own_ref = f32[1,1,2,128,128]{4,3,2,1,0:T(8,128)S(1)} collective-permute-done((f32[1,1,2,128,128]{4,3,2,1,0:T(8,128)S(1)}, f32[1,1,2,128,128]{4,3,2,1,0:T(8,128)S(1)}, u32[]{:S(2)}, u32[]{:S(2)}) %collective-permute-start) | collective-permute-done | bytes 131104 | tf_op jit(solution)/shard_map/ppermute | solution.py:219
  10.1 1.7 %collective-permute-start.1 = (f32[1,1,2,128,128]{4,3,2,1,0:T(8,128)S(1)}, f32[1,1,2,128,128]{4,3,2,1,0:T(8,128)S(1)}, u32[]{:S(2)}, u32[]{:S(2)}) collective-permute-start(f32[1,1,2,128,128]{4,3,2,1,0:T(8,128)S(1)} %collective-permute-done.own_ref), channel_id=1, source_target_pairs={{0,1},{4,5},{8,9},{12,13},{16,17},{20,21},{24,25},{28,29},{1,0},{5... | collective-permute-start | bytes 393224 | tf_op jit(solution)/shard_map/ppermute | solution.py:219
  11.8 1.0 %collective-permute-start.2 = (f32[1,1,2,128,128]{4,3,2,1,0:T(8,128)S(1)}, f32[1,1,2,128,128]{4,3,2,1,0:T(8,128)S(1)}, u32[]{:S(2)}, u32[]{:S(2)}) collective-permute-start(f32[1,1,2,128,128]{4,3,2,1,0:T(8,128)S(1)} %collective-permute-done.own_ref), channel_id=1, source_target_pairs={{0,4},{4,0},{8,12},{12,8},{16,20},{20,16},{24,28},{28,24},{1,2},{5... | collective-permute-start | bytes 393224 | tf_op jit(solution)/shard_map/ppermute | solution.py:219
  12.7 0.0 collective-permute-done.3.even_ref
  12.7 0.0 collective-permute-done.4.odd_ref
  12.8 1.9 %shard_map.57 = (f32[1,1,2,128,128]{4,3,2,1,0:T(8,128)S(1)}, f32[2,1,2,128,128]{4,3,2,1,0:T(8,128)S(1)}, f32[2,1,2,128,128]{4,3,2,1,0:T(8,128)S(1)}) custom-call(f32[2,1,2,128,128]{4,3,2,1,0:T(8,128)S(1)} %copy-done.2, f32[2,1,2,128,128]{4,3,2,1,0:T(8,128)S(1)} %collective-permute-done.3.even_ref, f32[2,1,2,128,128]{4,3,2,1,0:T(8,128)S(1)} %collective-permute-done.4.odd_ref, ...), custom_call_target="tpu_custom_call" | custom-call | flops 10000000000 | tf_op jit(solution)/shard_map/pallas_call | solution.py:228
  14.7 1.0 %collective-permute-start.5 = (f32[1,1,2,128,128]{4,3,2,1,0:T(8,128)S(1)}, f32[1,1,2,128,128]{4,3,2,1,0:T(8,128)S(1)}, u32[]{:S(2)}, u32[]{:S(2)}) collective-permute-start(f32[1,1,2,128,128]{4,3,2,1,0:T(8,128)S(1)} %get-tuple-element.27), channel_id=1, source_target_pairs={{0,1},{1,0},{2,3},{3,2},{4,8},{5,9},{6,10},{7,11},{8,4},{9,5},{10,... | collective-permute-start | bytes 393224 | tf_op jit(solution)/shard_map/ppermute | solution.py:219
  15.7 1.8 %shard_map.58 = (f32[2,1,2,128,128]{4,3,2,1,0:T(8,128)S(1)}, f32[2,1,2,128,128]{4,3,2,1,0:T(8,128)S(1)}) custom-call(f32[2,1,2,128,128]{4,3,2,1,0:T(8,128)S(1)} %copy-done.2, f32[2,1,2,128,128]{4,3,2,1,0:T(8,128)S(1)} %collective-permute-done.3.even_ref, f32[2,1,2,128,128]{4,3,2,1,0:T(8,128)S(1)} %collective-permute-done.4.odd_ref, ...), custom_call_target="tpu_custom_call" | custom-call | flops 10000000000 | tf_op jit(solution)/shard_map/pallas_call | solution.py:228
  17.6 2.2 %collective-permute-start.6 = (f32[2,1,2,128,128]{4,3,2,1,0:T(8,128)S(1)}, f32[2,1,2,128,128]{4,3,2,1,0:T(8,128)S(1)}, u32[]{:S(2)}, u32[]{:S(2)}) collective-permute-start(f32[2,1,2,128,128]{4,3,2,1,0:T(8,128)S(1)} %get-tuple-element.28), channel_id=1, source_target_pairs={{0,4},{1,5},{2,6},{3,7},{4,0},{5,1},{6,2},{7,3},{8,12},{9,13},{10,... | collective-permute-start | bytes 786440 | tf_op jit(solution)/shard_map/ppermute | solution.py:219
  19.8 0.0 collective-permute-done.1.even_ref
  19.8 0.0 collective-permute-done.2.odd_ref
  19.8 1.8 %shard_map.59.before = f32[2,1,2,128,128]{4,3,2,1,0:T(8,128)S(1)} custom-call(f32[1,1,2,128,128]{4,3,2,1,0:T(8,128)S(1)} %collective-permute-done.own_ref, f32[1,1,2,128,128]{4,3,2,1,0:T(8,128)S(1)} %collective-permute-done.1.even_ref, f32[1,1,2,128,128]{4,3,2,1,0:T(8,128)S(1)} %collective-permute-done.2.odd_ref, f32[3,8,256]{2,1,0:T(8,128)S(1)} %get-tuple-element.17.is_own, ...), custom_call_target="tpu_custom_call" | custom-call | tf_op jit(solution)/shard_map/pallas_call | solution.py:228
  21.7 0.0 collective-permute-done.5.got_odd_ref
  21.7 0.0 collective-permute-done.6.got_even_ref
  21.7 0.7 %shard_map.61 = f32[2,1,2,128,128]{4,3,2,1,0:T(8,128)} custom-call(f32[2,1,2,128,128]{4,3,2,1,0:T(8,128)S(1)} %shard_map.60.stay_ref, f32[2,1,2,128,128]{4,3,2,1,0:T(8,128)S(1)} %collective-permute-done.6.got_even_ref), custom_call_target="tpu_custom_call" | custom-call | flops 1000000000 | tf_op jit(solution)/shard_map/pallas_call | solution.py:228
  (9 shorter events, 0.0 us)
Async XLA Ops:
  0.0 5.4 %copy-start = (f32[4,1,3,2,128,128]{5,4,3,2,1,0:T(8,128)S(1)}, f32[4,1,3,2,128,128]{5,4,3,2,1,0:T(8,128)}, u32[]{:S(2)}) copy-start(f32[4,1,3,2,128,128]{5,4,3,2,1,0:T(8,128)} %couple_ref.1) | copy-start | bytes 4718596
  0.0 12.7 %collective-permute-start.3 = (f32[2,1,2,128,128]{4,3,2,1,0:T(8,128)}, f32[2,1,2,128,128]{4,3,2,1,0:T(8,128)S(1)}, u32[]{:S(2)}, u32[]{:S(2)}) collective-permute-start(f32[2,1,2,128,128]{4,3,2,1,0:T(8,128)} %own_ref.5), channel_id=1, source_target_pairs={{0,1},{4,5},{8,9},{12,13},{16,17},{20,21},{24,25},{28,29},{1,0},{5... | collective-permute-start | bytes 786440 | tf_op jit(solution)/shard_map/ppermute | solution.py:219
  2.1 10.6 %collective-permute-start.4 = (f32[2,1,2,128,128]{4,3,2,1,0:T(8,128)}, f32[2,1,2,128,128]{4,3,2,1,0:T(8,128)S(1)}, u32[]{:S(2)}, u32[]{:S(2)}) collective-permute-start(f32[2,1,2,128,128]{4,3,2,1,0:T(8,128)} %own_ref.5), channel_id=1, source_target_pairs={{0,4},{4,0},{8,12},{12,8},{16,20},{20,16},{24,28},{28,24},{1,2},{5... | collective-permute-start | bytes 786440 | tf_op jit(solution)/shard_map/ppermute | solution.py:219
  3.1 0.9 %copy-start.1 = (f32[2,1,2,128,128]{4,3,2,1,0:T(8,128)S(1)}, f32[2,1,2,128,128]{4,3,2,1,0:T(8,128)}, u32[]{:S(2)}) copy-start(f32[2,1,2,128,128]{4,3,2,1,0:T(8,128)} %own_ref.5) | copy-start | bytes 786436
  4.0 1.4 %copy-start.3 = (s32[4]{0:T(128)S(1)}, s32[4]{0:T(128)}, u32[]{:S(2)}) copy-start(s32[4]{0:T(128)} %shifts_hbm.1) | copy-start | bytes 52
  4.0 1.4 %copy-start.4 = (f32[4]{0:T(128)S(1)}, f32[4]{0:T(128)}, u32[]{:S(2)}) copy-start(f32[4]{0:T(128)} %occupation_hbm.1) | copy-start | bytes 52
  4.0 1.4 %copy-start.5 = (s32[1,3]{1,0:T(1,128)S(1)}, s32[1,3]{1,0:T(1,128)}, u32[]{:S(2)}) copy-start(s32[1,3]{1,0:T(1,128)} %neighbours_hbm.1) | copy-start | bytes 40
  4.2 8.5 %copy-start.2 = (f32[2,1,2,128,128]{4,3,2,1,0:T(8,128)S(1)}, f32[2,1,2,128,128]{4,3,2,1,0:T(8,128)}, u32[]{:S(2)}) copy-start(f32[2,1,2,128,128]{4,3,2,1,0:T(8,128)} %own_ref.5) | copy-start | bytes 786436
  4.2 5.9 %collective-permute-start = (f32[1,1,2,128,128]{4,3,2,1,0:T(8,128)S(1)}, f32[1,1,2,128,128]{4,3,2,1,0:T(8,128)S(1)}, u32[]{:S(2)}, u32[]{:S(2)}) collective-permute-start(f32[1,1,2,128,128]{4,3,2,1,0:T(8,128)S(1)} %shard_map.55), channel_id=1, source_target_pairs={{0,1},{1,0},{2,3},{3,2},{4,8},{5,9},{6,10},{7,11},{8,4},{9,5},{10,... | collective-permute-start | bytes 393224 | tf_op jit(solution)/shard_map/ppermute | solution.py:219
  10.1 9.7 %collective-permute-start.1 = (f32[1,1,2,128,128]{4,3,2,1,0:T(8,128)S(1)}, f32[1,1,2,128,128]{4,3,2,1,0:T(8,128)S(1)}, u32[]{:S(2)}, u32[]{:S(2)}) collective-permute-start(f32[1,1,2,128,128]{4,3,2,1,0:T(8,128)S(1)} %collective-permute-done.own_ref), channel_id=1, source_target_pairs={{0,1},{4,5},{8,9},{12,13},{16,17},{20,21},{24,25},{28,29},{1,0},{5... | collective-permute-start | bytes 393224 | tf_op jit(solution)/shard_map/ppermute | solution.py:219
  11.8 8.1 %collective-permute-start.2 = (f32[1,1,2,128,128]{4,3,2,1,0:T(8,128)S(1)}, f32[1,1,2,128,128]{4,3,2,1,0:T(8,128)S(1)}, u32[]{:S(2)}, u32[]{:S(2)}) collective-permute-start(f32[1,1,2,128,128]{4,3,2,1,0:T(8,128)S(1)} %collective-permute-done.own_ref), channel_id=1, source_target_pairs={{0,4},{4,0},{8,12},{12,8},{16,20},{20,16},{24,28},{28,24},{1,2},{5... | collective-permute-start | bytes 393224 | tf_op jit(solution)/shard_map/ppermute | solution.py:219
  14.7 7.0 %collective-permute-start.5 = (f32[1,1,2,128,128]{4,3,2,1,0:T(8,128)S(1)}, f32[1,1,2,128,128]{4,3,2,1,0:T(8,128)S(1)}, u32[]{:S(2)}, u32[]{:S(2)}) collective-permute-start(f32[1,1,2,128,128]{4,3,2,1,0:T(8,128)S(1)} %get-tuple-element.27), channel_id=1, source_target_pairs={{0,1},{1,0},{2,3},{3,2},{4,8},{5,9},{6,10},{7,11},{8,4},{9,5},{10,... | collective-permute-start | bytes 393224 | tf_op jit(solution)/shard_map/ppermute | solution.py:219
  17.6 4.2 %collective-permute-start.6 = (f32[2,1,2,128,128]{4,3,2,1,0:T(8,128)S(1)}, f32[2,1,2,128,128]{4,3,2,1,0:T(8,128)S(1)}, u32[]{:S(2)}, u32[]{:S(2)}) collective-permute-start(f32[2,1,2,128,128]{4,3,2,1,0:T(8,128)S(1)} %get-tuple-element.28), channel_id=1, source_target_pairs={{0,4},{1,5},{2,6},{3,7},{4,0},{5,1},{6,2},{7,3},{8,12},{9,13},{10,... | collective-permute-start | bytes 786440 | tf_op jit(solution)/shard_map/ppermute | solution.py:219

commit v4 on v3

--- a/solution.py
+++ b/solution.py
@@ -2,6 +2,7 @@
 
 import jax
 import jax.numpy as jnp
+import numpy as np
 from jax import lax
 from jax.experimental import pallas as pl
 from jax.experimental.pallas import tpu as pltpu
@@ -11,19 +12,19 @@
 ROWS = 8
 
 
-def neighbour_pairs(mesh, axis, other, odd):
-    count, count_other = mesh.shape[axis], mesh.shape[other]
+def neighbour_pairs(mesh, axis, odd, other=None):
+    count = mesh.shape[axis]
     axes = tuple(mesh.axis_names)
+    flat = lambda at: at[axes[0]] * mesh.shape[axes[1]] + at[axes[1]]
     pairs = []
-    for here in range(count):
-        there = here ^ 1 if not odd else ((here + 1) ^ 1) - 1
-        for side in range(count_other):
-            inside = 0 <= there < count
-            source = {axis: here, other: side}
-            target = {axis: there, other: side} if inside else {axis: here, other: side ^ 1}
-            if target[other] < count_other:
-                flat = [at[axes[0]] * mesh.shape[axes[1]] + at[axes[1]] for at in (source, target)]
-                pairs.append((flat[0], flat[1]))
+    for place in np.ndindex(*(mesh.shape[name] for name in axes)):
+        here = dict(zip(axes, place))
+        partner = here[axis] ^ 1 if not odd else ((here[axis] + 1) ^ 1) - 1
+        if other is not None and not 0 <= partner < count:
+            there = {**here, other: here[other] ^ 1}
+        else:
+            there = {**here, axis: partner % count}
+        pairs.append((flat(here), flat(there)))
     return axes, pairs
 
 
@@ -161,6 +162,10 @@
         put(give_more_ref, index, totals.get(energies + index, zero))
 
 
+def pass_kernel(foreign_ref, after_ref, out_ref):
+    out_ref[...] = foreign_ref[...]
+
+
 def near_far_kernel(
     own_ref, even_ref, odd_ref, is_own, is_even, up, lead, back, stay_before, give_before, stay_ref, give_ref, embeds
 ):
@@ -216,8 +221,8 @@
     energies, _, _, size, _ = green_lesser.shape
     modes, _, blocks = coupling.shape[:3]
     ends = mesh.shape["energy"] - 1
-    swap = lambda value, axis, other, odd: lax.ppermute(value, *neighbour_pairs(mesh, axis, other, odd))
-    slabs = lambda value: [swap(value, "slab", "energy", odd) for odd in (False, True)]
+    swap = lambda value, *how: lax.ppermute(value, *neighbour_pairs(mesh, *how))
+    slabs = lambda value: [swap(value, "slab", odd, "energy") for odd in (False, True)]
     vmem = pl.BlockSpec(memory_space=pltpu.VMEM)
     hbm = pl.BlockSpec(memory_space=pltpu.HBM)
     half = lambda *shape: jax.ShapeDtypeStruct(shape, jnp.bfloat16)
@@ -237,8 +242,7 @@
 
     slab_own = slabs(green_lesser)
     (near,) = call(near_kernel, [block(1)], [hbm], [green_lesser], 2, 10, scratch_shapes=[pltpu.SemaphoreType.DMA])
-    foreign = swap(near, "energy", "slab", True)
-    slab_foreign = slabs(foreign)
+    foreign = swap(near, "energy", True)
     wide = (ROWS, 2 * size)
     lead, back, is_own, is_even, down, up, foreign_up = call(
         functools.partial(prepare_kernel, ends, energies),
@@ -257,12 +261,14 @@
         far_kernel, [block(energies - 1), block(energies), block(energies)], [vmem] * 9,
         [green_lesser, *slab_own, is_own, is_even, down, up, lead, back], 8, 10, scratch_shapes=embeds,
     )
-    got_odd = swap(give_odd, "energy", "slab", True)
+    (foreign,) = call(pass_kernel, [block(1)], [vmem] * 2, [foreign, stay], 2, 1)
+    slab_foreign = slabs(foreign)
+    got_odd = swap(give_odd, "energy", True)
     stay, give_even = call(
         near_far_kernel, [block(energies)] * 2, [vmem] * 10,
         [green_lesser, *slab_own, is_own, is_even, up, lead, back, stay, give_even], 8, 10, scratch_shapes=embeds,
     )
-    got_even = swap(give_even, "energy", "slab", False)
+    got_even = swap(give_even, "energy", False)
     (stay,) = call(
         foreign_kernel, [block(energies)], [vmem] * 9,
         [foreign, *slab_foreign, is_own, is_even, foreign_up, lead, back, stay], 8, 0, scratch_shapes=embeds,

time: 22.6 us -> 21.8 us (0.965)
  waiting for transfers between devices: 3.48 us -> 1.76 us
  starting transfers between devices: 10.2 us -> 11.1 us
    ppermute x7, waiting for transfers between devices: 3.48 us -> 1.76 us  [shards(): swap = lambda value, *how: lax.ppermute(value, *neighbour_pairs(mesh, *how))]
    ppermute x7, starting transfers between devices: 10.2 us -> 11.1 us  [shards(): swap = lambda value, *how: lax.ppermute(value, *neighbour_pairs(mesh, *how))]
    pallas_call x7 -> x8, Pallas kernels: 7.73 us -> 7.72 us  [call(): pl.pallas_call(kernel, out_shape=outs, in_specs=ins, out_specs=more.pop('...]
  transfers between devices with their start and end apart: 7 -> 7, of which waited for: 1 -> 1; matrix products, arithmetic and copies ran while one was open for 0% -> 0% of each run, Pallas kernels for 31% -> 32%
where the time goes in v4:
time: 21.8 us; the launch traced here: 21.6 us
  starting transfers between devices  11.1 us (51%)
  Pallas kernels  7.72 us (35%)
  waiting for transfers between devices  1.76 us (8%)
  local copies, waits for them, and re-layouts  0.97 us (4%)
    ppermute x7, starting transfers between devices, shards(): swap = lambda value, *how: lax.ppermute(value, *neighbour_pairs(mesh, *how))  11.1 us
    pallas_call x8, Pallas kernels, call(): pl.pallas_call(kernel, out_shape=outs, in_specs=ins, out_specs=more.pop('...  7.72 us
    ppermute x7, waiting for transfers between devices, shards(): swap = lambda value, *how: lax.ppermute(value, *neighbour_pairs(mesh, *how))  1.76 us
    unnamed x12, local copies, waits for them, and re-layouts  0.97 us
  transfers between devices with their start and end apart: 7, of which 1 were waited for; matrix products, arithmetic and copies ran while one was open for 0% of the time, Pallas kernels for 32%

profile of v4, /device:TPU:1, one launch (start us, length us, event | category | flops | bytes accessed | tf_op | source)
XLA Modules:
  0.0 21.6 jit_solution(7587514370296793365)
XLA Ops:
  0.0 2.1 %collective-permute-start.1 = (f32[2,1,2,128,128]{4,3,2,1,0:T(8,128)}, f32[2,1,2,128,128]{4,3,2,1,0:T(8,128)S(1)}, u32[]{:S(2)}, u32[]{:S(2)}) collective-permute-start(f32[2,1,2,128,128]{4,3,2,1,0:T(8,128)} %own_ref.5), channel_id=1, source_target_pairs={{0,1},{1,0},{2,3},{3,2},{4,5},{5,4},{6,7},{7,6},{8,9},{9,8},{10,11... | collective-permute-start | bytes 786440 | tf_op jit(solution)/shard_map/ppermute | solution.py:224
  2.1 1.0 %collective-permute-start.2 = (f32[2,1,2,128,128]{4,3,2,1,0:T(8,128)}, f32[2,1,2,128,128]{4,3,2,1,0:T(8,128)S(1)}, u32[]{:S(2)}, u32[]{:S(2)}) collective-permute-start(f32[2,1,2,128,128]{4,3,2,1,0:T(8,128)} %own_ref.5), channel_id=1, source_target_pairs={{0,4},{1,2},{2,1},{3,7},{4,0},{5,6},{6,5},{7,3},{8,12},{9,10},{10,... | collective-permute-start | bytes 786440 | tf_op jit(solution)/shard_map/ppermute | solution.py:224
  3.1 0.9 %copy-done.1 = f32[2,1,2,128,128]{4,3,2,1,0:T(8,128)S(1)} copy-done((f32[2,1,2,128,128]{4,3,2,1,0:T(8,128)S(1)}, f32[2,1,2,128,128]{4,3,2,1,0:T(8,128)}, u32[]{:S(2)}) %copy-start.1) | copy-done | bytes 262168
  4.0 0.2 shard_map.55
  4.2 0.0 copy-start.2
  4.2 1.2 %collective-permute-start = (f32[1,1,2,128,128]{4,3,2,1,0:T(8,128)S(1)}, f32[1,1,2,128,128]{4,3,2,1,0:T(8,128)S(1)}, u32[]{:S(2)}, u32[]{:S(2)}) collective-permute-start(f32[1,1,2,128,128]{4,3,2,1,0:T(8,128)S(1)} %shard_map.55), channel_id=1, source_target_pairs={{0,28},{1,29},{2,30},{3,31},{4,8},{5,9},{6,10},{7,11},{8,4},{9,5},... | collective-permute-start | bytes 393224 | tf_op jit(solution)/shard_map/ppermute | solution.py:224
  5.4 0.0 copy-done.3
  5.4 0.0 copy-done.5
  5.4 1.2 %shard_map.56 = (bf16[3,2,512,256]{3,2,1,0:T(8,128)(2,1)S(1)}, bf16[4,3,2,256,256]{4,3,2,1,0:T(8,128)(2,1)S(1)}, f32[3,8,256]{2,1,0:T(8,128)S(1)}, f32[3,8,256]{...) custom-call(s32[4]{0:T(128)S(1)} %copy-done.3, ...), custom_call_target="tpu_custom_call" | custom-call | flops 2000000000 | tf_op jit(solution)/shard_map/pallas_call | solution.py:233
  6.6 1.7 %collective-permute-done.1.even_ref = f32[2,1,2,128,128]{4,3,2,1,0:T(8,128)S(1)} collective-permute-done((f32[2,1,2,128,128]{4,3,2,1,0:T(8,128)}, f32[2,1,2,128,128]{4,3,2,1,0:T(8,128)S(1)}, u32[]{:S(2)}, u32[]{:S(2)}) %collective-permute-start.1) | collective-permute-done | bytes 262176 | tf_op jit(solution)/shard_map/ppermute | solution.py:224
  8.4 0.0 collective-permute-done.2.odd_ref
  8.4 1.9 %shard_map.57 = (f32[1,1,2,128,128]{4,3,2,1,0:T(8,128)S(1)}, f32[2,1,2,128,128]{4,3,2,1,0:T(8,128)S(1)}, f32[2,1,2,128,128]{4,3,2,1,0:T(8,128)S(1)}) custom-call(f32[2,1,2,128,128]{4,3,2,1,0:T(8,128)S(1)} %copy-done.2, f32[2,1,2,128,128]{4,3,2,1,0:T(8,128)S(1)} %collective-permute-done.1.even_ref, f32[2,1,2,128,128]{4,3,2,1,0:T(8,128)S(1)} %collective-permute-done.2.odd_ref, ...), custom_call_target="tpu_custom_call" | custom-call | flops 10000000000 | tf_op jit(solution)/shard_map/pallas_call | solution.py:233
  10.3 0.0 collective-permute-done.foreign_ref
  10.3 2.4 %collective-permute-start.3 = (f32[1,1,2,128,128]{4,3,2,1,0:T(8,128)S(1)}, f32[1,1,2,128,128]{4,3,2,1,0:T(8,128)S(1)}, u32[]{:S(2)}, u32[]{:S(2)}) collective-permute-start(f32[1,1,2,128,128]{4,3,2,1,0:T(8,128)S(1)} %shard_map.58.own_ref), channel_id=1, source_target_pairs={{0,1},{1,0},{2,3},{3,2},{4,5},{5,4},{6,7},{7,6},{8,9},{9,8},{10,11... | collective-permute-start | bytes 393224 | tf_op jit(solution)/shard_map/ppermute | solution.py:224
  12.7 1.8 %collective-permute-start.4 = (f32[1,1,2,128,128]{4,3,2,1,0:T(8,128)S(1)}, f32[1,1,2,128,128]{4,3,2,1,0:T(8,128)S(1)}, u32[]{:S(2)}, u32[]{:S(2)}) collective-permute-start(f32[1,1,2,128,128]{4,3,2,1,0:T(8,128)S(1)} %shard_map.58.own_ref), channel_id=1, source_target_pairs={{0,4},{1,2},{2,1},{3,7},{4,0},{5,6},{6,5},{7,3},{8,12},{9,10},{10,... | collective-permute-start | bytes 393224 | tf_op jit(solution)/shard_map/ppermute | solution.py:224
  14.5 1.1 %collective-permute-start.5 = (f32[1,1,2,128,128]{4,3,2,1,0:T(8,128)S(1)}, f32[1,1,2,128,128]{4,3,2,1,0:T(8,128)S(1)}, u32[]{:S(2)}, u32[]{:S(2)}) collective-permute-start(f32[1,1,2,128,128]{4,3,2,1,0:T(8,128)S(1)} %get-tuple-element.27), channel_id=1, source_target_pairs={{0,28},{1,29},{2,30},{3,31},{4,8},{5,9},{6,10},{7,11},{8,4},{9,5},... | collective-permute-start | bytes 393224 | tf_op jit(solution)/shard_map/ppermute | solution.py:224
  15.6 1.8 %shard_map.59 = (f32[2,1,2,128,128]{4,3,2,1,0:T(8,128)S(1)}, f32[2,1,2,128,128]{4,3,2,1,0:T(8,128)S(1)}) custom-call(f32[2,1,2,128,128]{4,3,2,1,0:T(8,128)S(1)} %copy-done.2, f32[2,1,2,128,128]{4,3,2,1,0:T(8,128)S(1)} %collective-permute-done.1.even_ref, f32[2,1,2,128,128]{4,3,2,1,0:T(8,128)S(1)} %collective-permute-done.2.odd_ref, ...), custom_call_target="tpu_custom_call" | custom-call | flops 10000000000 | tf_op jit(solution)/shard_map/pallas_call | solution.py:233
  17.5 1.5 %collective-permute-start.6 = (f32[2,1,2,128,128]{4,3,2,1,0:T(8,128)S(1)}, f32[2,1,2,128,128]{4,3,2,1,0:T(8,128)S(1)}, u32[]{:S(2)}, u32[]{:S(2)}) collective-permute-start(f32[2,1,2,128,128]{4,3,2,1,0:T(8,128)S(1)} %get-tuple-element.28), channel_id=1, source_target_pairs={{0,4},{1,5},{2,6},{3,7},{4,0},{5,1},{6,2},{7,3},{8,12},{9,13},{10,... | collective-permute-start | bytes 786440 | tf_op jit(solution)/shard_map/ppermute | solution.py:224
  19.0 0.0 collective-permute-done.3.even_ref
  19.0 0.0 collective-permute-done.4.odd_ref
  19.0 1.8 %shard_map.60.before = f32[2,1,2,128,128]{4,3,2,1,0:T(8,128)S(1)} custom-call(f32[1,1,2,128,128]{4,3,2,1,0:T(8,128)S(1)} %shard_map.58.own_ref, f32[1,1,2,128,128]{4,3,2,1,0:T(8,128)S(1)} %collective-permute-done.3.even_ref, f32[1,1,2,128,128]{4,3,2,1,0:T(8,128)S(1)} %collective-permute-done.4.odd_ref, f32[3,8,256]{2,1,0:T(8,128)S(1)} %get-tuple-element.17.is_own, ...), custom_call_target="tpu_custom_call" | custom-call | tf_op jit(solution)/shard_map/pallas_call | solution.py:233
  20.8 0.0 collective-permute-done.5.got_odd_ref
  20.9 0.0 collective-permute-done.6.got_even_ref
  20.9 0.7 %shard_map.62 = f32[2,1,2,128,128]{4,3,2,1,0:T(8,128)} custom-call(f32[2,1,2,128,128]{4,3,2,1,0:T(8,128)S(1)} %shard_map.61.stay_ref, f32[2,1,2,128,128]{4,3,2,1,0:T(8,128)S(1)} %collective-permute-done.6.got_even_ref), custom_call_target="tpu_custom_call" | custom-call | flops 1000000000 | tf_op jit(solution)/shard_map/pallas_call | solution.py:233
  (10 shorter events, 0.1 us)
Async XLA Ops:
  0.0 5.4 %copy-start = (f32[4,1,3,2,128,128]{5,4,3,2,1,0:T(8,128)S(1)}, f32[4,1,3,2,128,128]{5,4,3,2,1,0:T(8,128)}, u32[]{:S(2)}) copy-start(f32[4,1,3,2,128,128]{5,4,3,2,1,0:T(8,128)} %couple_ref.1) | copy-start | bytes 4718596
  0.0 8.4 %collective-permute-start.1 = (f32[2,1,2,128,128]{4,3,2,1,0:T(8,128)}, f32[2,1,2,128,128]{4,3,2,1,0:T(8,128)S(1)}, u32[]{:S(2)}, u32[]{:S(2)}) collective-permute-start(f32[2,1,2,128,128]{4,3,2,1,0:T(8,128)} %own_ref.5), channel_id=1, source_target_pairs={{0,1},{1,0},{2,3},{3,2},{4,5},{5,4},{6,7},{7,6},{8,9},{9,8},{10,11... | collective-permute-start | bytes 786440 | tf_op jit(solution)/shard_map/ppermute | solution.py:224
  2.1 6.2 %collective-permute-start.2 = (f32[2,1,2,128,128]{4,3,2,1,0:T(8,128)}, f32[2,1,2,128,128]{4,3,2,1,0:T(8,128)S(1)}, u32[]{:S(2)}, u32[]{:S(2)}) collective-permute-start(f32[2,1,2,128,128]{4,3,2,1,0:T(8,128)} %own_ref.5), channel_id=1, source_target_pairs={{0,4},{1,2},{2,1},{3,7},{4,0},{5,6},{6,5},{7,3},{8,12},{9,10},{10,... | collective-permute-start | bytes 786440 | tf_op jit(solution)/shard_map/ppermute | solution.py:224
  3.1 0.9 %copy-start.1 = (f32[2,1,2,128,128]{4,3,2,1,0:T(8,128)S(1)}, f32[2,1,2,128,128]{4,3,2,1,0:T(8,128)}, u32[]{:S(2)}) copy-start(f32[2,1,2,128,128]{4,3,2,1,0:T(8,128)} %own_ref.5) | copy-start | bytes 786436
  4.0 1.4 %copy-start.3 = (s32[4]{0:T(128)S(1)}, s32[4]{0:T(128)}, u32[]{:S(2)}) copy-start(s32[4]{0:T(128)} %shifts_hbm.1) | copy-start | bytes 52
  4.0 1.4 %copy-start.4 = (f32[4]{0:T(128)S(1)}, f32[4]{0:T(128)}, u32[]{:S(2)}) copy-start(f32[4]{0:T(128)} %occupation_hbm.1) | copy-start | bytes 52
  4.0 1.4 %copy-start.5 = (s32[1,3]{1,0:T(1,128)S(1)}, s32[1,3]{1,0:T(1,128)}, u32[]{:S(2)}) copy-start(s32[1,3]{1,0:T(1,128)} %neighbours_hbm.1) | copy-start | bytes 40
  4.2 4.2 %copy-start.2 = (f32[2,1,2,128,128]{4,3,2,1,0:T(8,128)S(1)}, f32[2,1,2,128,128]{4,3,2,1,0:T(8,128)}, u32[]{:S(2)}) copy-start(f32[2,1,2,128,128]{4,3,2,1,0:T(8,128)} %own_ref.5) | copy-start | bytes 786436
  4.2 6.1 %collective-permute-start = (f32[1,1,2,128,128]{4,3,2,1,0:T(8,128)S(1)}, f32[1,1,2,128,128]{4,3,2,1,0:T(8,128)S(1)}, u32[]{:S(2)}, u32[]{:S(2)}) collective-permute-start(f32[1,1,2,128,128]{4,3,2,1,0:T(8,128)S(1)} %shard_map.55), channel_id=1, source_target_pairs={{0,28},{1,29},{2,30},{3,31},{4,8},{5,9},{6,10},{7,11},{8,4},{9,5},... | collective-permute-start | bytes 393224 | tf_op jit(solution)/shard_map/ppermute | solution.py:224
  10.3 8.7 %collective-permute-start.3 = (f32[1,1,2,128,128]{4,3,2,1,0:T(8,128)S(1)}, f32[1,1,2,128,128]{4,3,2,1,0:T(8,128)S(1)}, u32[]{:S(2)}, u32[]{:S(2)}) collective-permute-start(f32[1,1,2,128,128]{4,3,2,1,0:T(8,128)S(1)} %shard_map.58.own_ref), channel_id=1, source_target_pairs={{0,1},{1,0},{2,3},{3,2},{4,5},{5,4},{6,7},{7,6},{8,9},{9,8},{10,11... | collective-permute-start | bytes 393224 | tf_op jit(solution)/shard_map/ppermute | solution.py:224
  12.7 6.3 %collective-permute-start.4 = (f32[1,1,2,128,128]{4,3,2,1,0:T(8,128)S(1)}, f32[1,1,2,128,128]{4,3,2,1,0:T(8,128)S(1)}, u32[]{:S(2)}, u32[]{:S(2)}) collective-permute-start(f32[1,1,2,128,128]{4,3,2,1,0:T(8,128)S(1)} %shard_map.58.own_ref), channel_id=1, source_target_pairs={{0,4},{1,2},{2,1},{3,7},{4,0},{5,6},{6,5},{7,3},{8,12},{9,10},{10,... | collective-permute-start | bytes 393224 | tf_op jit(solution)/shard_map/ppermute | solution.py:224
  14.5 6.3 %collective-permute-start.5 = (f32[1,1,2,128,128]{4,3,2,1,0:T(8,128)S(1)}, f32[1,1,2,128,128]{4,3,2,1,0:T(8,128)S(1)}, u32[]{:S(2)}, u32[]{:S(2)}) collective-permute-start(f32[1,1,2,128,128]{4,3,2,1,0:T(8,128)S(1)} %get-tuple-element.27), channel_id=1, source_target_pairs={{0,28},{1,29},{2,30},{3,31},{4,8},{5,9},{6,10},{7,11},{8,4},{9,5},... | collective-permute-start | bytes 393224 | tf_op jit(solution)/shard_map/ppermute | solution.py:224
  17.5 3.4 %collective-permute-start.6 = (f32[2,1,2,128,128]{4,3,2,1,0:T(8,128)S(1)}, f32[2,1,2,128,128]{4,3,2,1,0:T(8,128)S(1)}, u32[]{:S(2)}, u32[]{:S(2)}) collective-permute-start(f32[2,1,2,128,128]{4,3,2,1,0:T(8,128)S(1)} %get-tuple-element.28), channel_id=1, source_target_pairs={{0,4},{1,5},{2,6},{3,7},{4,0},{5,1},{6,2},{7,3},{8,12},{9,13},{10,... | collective-permute-start | bytes 786440 | tf_op jit(solution)/shard_map/ppermute | solution.py:224

commit v5 on v4

v5 whole, which is shorter than its diff:
```python
import functools

import jax
import jax.numpy as jnp
import numpy as np
from jax import lax
from jax.experimental import pallas as pl
from jax.experimental.pallas import tpu as pltpu
from jax.sharding import PartitionSpec as P

BYTES = 1 << 20
ROWS = 8


def neighbour_pairs(mesh, axis, odd, other=None):
    count = mesh.shape[axis]
    axes = tuple(mesh.axis_names)
    flat = lambda at: at[axes[0]] * mesh.shape[axes[1]] + at[axes[1]]
    pairs = []
    for place in np.ndindex(*(mesh.shape[name] for name in axes)):
        here = dict(zip(axes, place))
        partner = here[axis] ^ 1 if not odd else ((here[axis] + 1) ^ 1) - 1
        if other is not None and not 0 <= partner < count:
            there = {**here, other: here[other] ^ 1}
        else:
            there = {**here, axis: partner % count}
        pairs.append((flat(here), flat(there)))
    return axes, pairs


def even_place():
    return lax.rem(lax.axis_index("energy"), 2) == 0


def row_of(number, energies):
    return jnp.where(even_place(), number, energies - 1 - number)


def split(value):
    high = value.astype(jnp.bfloat16)
    return high, (value - high.astype(jnp.float32)).astype(jnp.bfloat16)


def product(lead_high, lead_low, trail_high, trail_low):
    dot = functools.partial(jnp.dot, preferred_element_type=jnp.float32)
    return dot(lead_high, trail_high) + (dot(lead_low, trail_high) + dot(lead_high, trail_low))


def embed(target, index, real, imag, size):
    for part, (real_part, imag_part) in enumerate(zip(split(real), split(imag))):
        target[*index, part, :size, :size] = real_part
        target[*index, part, :size, size:] = imag_part
        target[*index, part, size:, :size] = -imag_part
        target[*index, part, size:, size:] = real_part


def pass_kernel(block_ref, out_ref):
    out_ref[...] = block_ref[...]


def prepare_kernel(
    energies, shifts_hbm, occupation_hbm, neighbours_hbm, couple_ref, far_ref,
    lead, back, is_own, is_even, down, up, far_out, shifts, occupation, neighbours, sems,
):
    modes, _, blocks, _, size, _ = couple_ref.shape
    copies = [
        pltpu.make_async_copy(source, target, sems.at[index])
        for index, (source, target) in enumerate(
            ((shifts_hbm, shifts), (occupation_hbm, occupation), (neighbours_hbm, neighbours))
        )
    ]
    for copy in copies:
        copy.start()
    far_out[...] = far_ref[...]
    for mode in range(modes):
        for block in range(blocks):
            real, imag = couple_ref[mode, 0, block, 0], couple_ref[mode, 0, block, 1]
            rows = slice(mode * size, (mode + 1) * size)
            for part, (real_part, imag_part) in enumerate(zip(split(real), split(imag))):
                lead[block, part, rows, :size] = real_part
                lead[block, part, rows, size:] = imag_part
            embed(back, (mode, block), real.T, -imag.T, size)
    for copy in copies:
        copy.wait()
    here = lax.axis_index("slab")
    ahead = 1 - 2 * lax.rem(here, 2)
    wide = (ROWS, 2 * size)
    for block in range(blocks):
        offset = neighbours[0, block] - here
        is_own[block] = jnp.full(wide, jnp.where(offset == 0, 1.0, 0.0), jnp.float32)
        is_even[block] = jnp.full(wide, jnp.where(offset == ahead, 1.0, 0.0), jnp.float32)
    for mode in range(modes):
        less, more = occupation[mode], occupation[mode] + 1.0
        down_weight = jnp.where(even_place(), more, less)
        up_weight = jnp.where(even_place(), less, more)
        for shift in range(1, energies + 1):
            chosen = shifts[mode] == shift
            for ref, weight in ((down, down_weight), (up, up_weight)):
                ref[mode, shift - 1] = jnp.full(wide, jnp.where(chosen, weight, 0.0), jnp.float32)


def scaled(value, weight):
    return (value.reshape(-1, ROWS, value.shape[1]) * weight[None]).reshape(value.shape)


def sandwiches(own, even, odd, is_own, is_even, lead, back, embeds):
    blocks, size = lead.shape[0], lead.shape[3] // 2
    middles = []
    for block in range(blocks):
        take_own = is_own[block][None, :, :size] != 0.0
        take_even = is_even[block][None, :, :size] != 0.0
        tiles = (size // ROWS, ROWS, size)
        parts = [
            jnp.where(
                take_own, own(part).reshape(tiles),
                jnp.where(take_even, even(part).reshape(tiles), odd(part).reshape(tiles)),
            ).reshape(size, size)
            for part in range(2)
        ]
        embed(embeds, (block,), *parts, size)
        middles.append(product(lead[block, 0], lead[block, 1], embeds[block, 0], embeds[block, 1]))
    for mode in range(back.shape[0]):
        rows = slice(mode * size, (mode + 1) * size)
        total = 0.0
        for block in range(blocks):
            high, low = split(middles[block][rows])
            total = total + product(high, low, back[mode, block, 0], back[mode, block, 1])
        yield mode, total


def put(ref, row, value, add=None):
    size = value.shape[0]
    for part in range(2):
        one = value[:, part * size : (part + 1) * size]
        ref[row, 0, part] = one if add is None else add[row, 0, part] + one


def near_kernel(
    own_ref, odd_ref, even_ref, is_own, is_even, down, up, lead, back, give_ref, border_ref, stay_ref, mate_ref, embeds
):
    energies = stay_ref.shape[0]
    reader = lambda ref: lambda part: ref[0, 0, part]
    totals = {}
    for mode, value in sandwiches(
        reader(own_ref), reader(even_ref), reader(odd_ref), is_own, is_even, lead, back, embeds
    ):
        for shift in range(1, energies + 1):
            for target, weights in ((-shift, down), (shift, up)):
                totals[target] = totals.get(target, 0.0) + scaled(value, weights[mode, shift - 1])
    put(give_ref, 0, totals[-energies])
    for index in range(energies - 1):
        put(border_ref, index, totals[-1 - index])
        put(stay_ref, index + 1, totals[index + 1])
    put(mate_ref, 0, totals[energies])


def far_kernel(
    own_ref, odd_ref, even_ref, is_own, is_even, down, up, lead, back, border, stay, mate,
    give_ref, stay_ref, mate_ref, embeds,
):
    energies = stay_ref.shape[0]
    totals = {}
    for number in range(1, energies):
        row = jnp.where(even_place(), number - 1, energies - 1 - number)
        reader = lambda ref: lambda part: ref[row, 0, part]
        for mode, value in sandwiches(
            reader(own_ref), reader(even_ref), reader(odd_ref), is_own, is_even, lead, back, embeds
        ):
            for shift in range(1, energies + 1):
                for target, weights in ((number - shift, down), (number + shift, up)):
                    totals[target] = totals.get(target, 0.0) + scaled(value, weights[mode, shift - 1])
    for index in range(energies - 1):
        put(give_ref, index, totals[-1 - index], border)
    for index in range(energies):
        if index in totals:
            put(stay_ref, index, totals[index], stay if index else None)
        else:
            stay_ref[index] = stay[index]
        put(mate_ref, index, totals[energies + index], None if index else mate)


def first_kernel(ends, stay_ref, got_first_ref, out_ref):
    energies = stay_ref.shape[0]
    place = lax.axis_index("energy")
    inside = jnp.logical_and(place != 0, place != ends)
    for number in range(energies - 1):
        out_ref[number] = stay_ref[number]
    out_ref[energies - 1] = stay_ref[energies - 1] + jnp.where(inside, got_first_ref[0], 0.0)


def sum_kernel(ends, stay_ref, got_rest_ref, got_even_ref, out_ref):
    energies = stay_ref.shape[0]
    place = lax.axis_index("energy")
    inside = jnp.logical_and(place != 0, place != ends)
    for number in range(energies):
        value = stay_ref[number] + got_even_ref[energies - 1 - number]
        if number < energies - 1:
            value += jnp.where(inside, got_rest_ref[number], 0.0)
        out_ref[row_of(number, energies)] = value


def shards(mesh, green_lesser, coupling, occupation, shifts, neighbours):
    energies, _, _, size, _ = green_lesser.shape
    modes, _, blocks = coupling.shape[:3]
    ends = mesh.shape["energy"] - 1
    swap = lambda value, *how: lax.ppermute(value, *neighbour_pairs(mesh, *how))
    slabs = lambda value: [swap(value, "slab", odd, "energy") for odd in (True, False)]
    vmem = pl.BlockSpec(memory_space=pltpu.VMEM)
    hbm = pl.BlockSpec(memory_space=pltpu.HBM)
    half = lambda *shape: jax.ShapeDtypeStruct(shape, jnp.bfloat16)
    full = lambda *shape: jax.ShapeDtypeStruct(shape, jnp.float32)
    block = lambda count: full(count, *green_lesser.shape[1:])

    def call(kernel, outs, ins, args, mib, micros, **more):
        return pl.pallas_call(
            kernel,
            out_shape=outs,
            in_specs=ins,
            out_specs=more.pop("out_specs", [vmem] * len(outs)),
            compiler_params=pltpu.CompilerParams(vmem_limit_bytes=mib * BYTES),
            cost_estimate=pl.CostEstimate(flops=micros * 10**9, bytes_accessed=0, transcendentals=0),
            **more,
        )(*args)

    near = lax.dynamic_slice_in_dim(green_lesser, row_of(0, energies), 1)
    (near,) = call(pass_kernel, [block(1)], [vmem], [near], 2, 10)
    near_slabs = slabs(near)
    near, green_lesser = lax.optimization_barrier((near, green_lesser))
    far = lax.dynamic_slice_in_dim(green_lesser, jnp.where(even_place(), 1, 0), energies - 1)
    wide = (ROWS, 2 * size)
    lead, back, is_own, is_even, down, up, far = call(
        functools.partial(prepare_kernel, energies),
        [half(blocks, 2, modes * size, 2 * size), half(modes, blocks, 2, 2 * size, 2 * size)]
        + [full(blocks, *wide)] * 2 + [full(modes, energies, *wide)] * 2 + [block(energies - 1)],
        [hbm] * 3 + [vmem] * 2, [shifts, occupation, neighbours, coupling, far], 8, 2,
        scratch_shapes=[
            pltpu.SMEM(shifts.shape, jnp.int32),
            pltpu.SMEM(occupation.shape, jnp.float32),
            pltpu.SMEM(neighbours.shape, jnp.int32),
            pltpu.SemaphoreType.DMA((3,)),
        ],
    )
    far_slabs = slabs(far)
    made = [is_own, is_even, down, up, lead, back]
    embeds = [pltpu.VMEM((blocks, 2, 2 * size, 2 * size), jnp.bfloat16)]
    give_first, border, stay, mate = call(
        near_kernel, [block(1), block(energies - 1), block(energies), block(1)], [vmem] * 9,
        [near, *near_slabs, *made], 8, 10, scratch_shapes=embeds,
    )
    got_first = swap(give_first, "energy", True, "slab")
    give_rest, stay, give_even = call(
        far_kernel, [block(energies - 1), block(energies), block(energies)], [vmem] * 12,
        [far, *far_slabs, *made, border, stay, mate], 8, 10, scratch_shapes=embeds,
    )
    got_rest = swap(give_rest, "energy", True, "slab")
    got_even = swap(give_even, "energy", False)
    (stay,) = call(functools.partial(first_kernel, ends), [block(energies)], [vmem] * 2, [stay, got_first], 2, 10)
    return call(
        functools.partial(sum_kernel, ends), block(energies), [vmem] * 3, [stay, got_rest, got_even], 4, 1,
        out_specs=pl.BlockSpec(green_lesser.shape, lambda: (0,) * green_lesser.ndim),
    )


def solution(mesh):
    placed = (
        P("energy", "slab", None, None, None),
        P(None, "slab", None, None, None, None),
        P(),
        P(),
        P("slab", None),
    )
    return jax.shard_map(
        functools.partial(shards, mesh),
        mesh=mesh,
        in_specs=placed,
        out_specs=P("energy", "slab", None, None, None),
        check_vma=False,
    )
```

time: 21.8 us -> 20.8 us (0.954)
  the two profiles are of different devices: /device:TPU:1 before, /device:TPU:0 now
where the time goes in v5:
time: 20.8 us; the launch traced here: 20.7 us
  starting transfers between devices  9.55 us (46%)
  Pallas kernels  5.45 us (26%)
  waiting for transfers between devices  4.54 us (22%)
  local copies, waits for them, and re-layouts  0.99 us (5%)
    ppermute x7, starting transfers between devices, shards(): swap = lambda value, *how: lax.ppermute(value, *neighbour_pairs(mesh, *how))  9.55 us
    pallas_call x6, Pallas kernels, call(): pl.pallas_call(kernel, out_shape=outs, in_specs=ins, out_specs=more.pop('...  5.45 us
    ppermute x7, waiting for transfers between devices, shards(): swap = lambda value, *how: lax.ppermute(value, *neighbour_pairs(mesh, *how))  4.54 us
    unnamed x10, local copies, waits for them, and re-layouts  0.98 us
  transfers between devices with their start and end apart: 7, of which 2 were waited for; matrix products, arithmetic and copies ran while one was open for 0% of the time, Pallas kernels for 23%

profile of v5, /device:TPU:0, one launch (start us, length us, event | category | flops | bytes accessed | tf_op | source)
XLA Modules:
  0.0 20.7 jit_solution(5800122772949164878)
XLA Ops:
  0.0 0.0 copy-start
  0.0 0.9 %copy-done = f32[2,1,2,128,128]{4,3,2,1,0:T(8,128)S(1)} copy-done((f32[2,1,2,128,128]{4,3,2,1,0:T(8,128)S(1)}, f32[2,1,2,128,128]{4,3,2,1,0:T(8,128)}, u32[]{:S(2)}) %copy-start) | copy-done | bytes 262168
  1.0 0.0 copy-start.1
  1.0 0.0 copy-start.2
  1.0 0.0 copy-start.3
  1.0 0.0 copy-start.4
  1.0 3.1 %collective-permute-start.3 = (f32[1,1,2,128,128]{4,3,2,1,0:T(8,128)S(1)}, f32[1,1,2,128,128]{4,3,2,1,0:T(8,128)S(1)}, u32[]{:S(2)}, u32[]{:S(2)}) collective-permute-start(f32[1,1,2,128,128]{4,3,2,1,0:T(8,128)S(1)} %shard_map.55.own_ref), channel_id=1, source_target_pairs={{0,1},{1,0},{2,3},{3,2},{4,5},{5,4},{6,7},{7,6},{8,9},{9,8},{10,11... | collective-permute-start | bytes 393224 | tf_op jit(solution)/shard_map/ppermute | solution.py:206
  4.1 0.0 collective-permute-start.2
  4.2 0.7 %shard_map.56 = (bf16[3,2,512,256]{3,2,1,0:T(8,128)(2,1)S(1)}, bf16[4,3,2,256,256]{4,3,2,1,0:T(8,128)(2,1)S(1)}, f32[3,8,256]{2,1,0:T(8,128)S(1)}, f32[3,8,256]{...) custom-call(s32[4]{0:T(128)S(1)} %copy-done.2, ...), custom_call_target="tpu_custom_call" | custom-call | flops 2000000000 | tf_op jit(solution)/shard_map/pallas_call | solution.py:215
  4.9 3.2 %collective-permute-start.1 = (f32[1,1,2,128,128]{4,3,2,1,0:T(8,128)S(1)}, f32[1,1,2,128,128]{4,3,2,1,0:T(8,128)S(1)}, u32[]{:S(2)}, u32[]{:S(2)}) collective-permute-start(f32[1,1,2,128,128]{4,3,2,1,0:T(8,128)S(1)} %get-tuple-element.22.own_ref), channel_id=1, source_target_pairs={{0,1},{1,0},{2,3},{3,2},{4,5},{5,4},{6,7},{7,6},{8,9},{9,8},{10,11... | collective-permute-start | bytes 393224 | tf_op jit(solution)/shard_map/ppermute | solution.py:206
  8.1 0.0 collective-permute-start
  8.1 0.0 collective-permute-done.3.even_ref
  8.1 0.0 collective-permute-done.2.odd_ref
  8.1 2.0 %shard_map.57 = (f32[1,1,2,128,128]{4,3,2,1,0:T(8,128)S(1)}, f32[1,1,2,128,128]{4,3,2,1,0:T(8,128)S(1)}, f32[2,1,2,128,128]{4,3,2,1,0:T(8,128)S(1)}, f32[1,1,2,128,128]{4,3,2,1,0:T(8,128)S(1)}) custom-call(f32[1,1,2,128,128]{4,3,2,1,0:T(8,128)S(1)} %shard_map.55.own_ref, f32[1,1,2,128,128]{4,3,2,1,0:T(8,128)S(1)} %collective-permute-done.2.odd_ref, ...), custom_call_target="tpu_custom_call" | custom-call | flops 10000000000 | tf_op jit(solution)/shard_map/pallas_call | solution.py:215
  10.1 2.8 %collective-permute-start.4 = (f32[1,1,2,128,128]{4,3,2,1,0:T(8,128)S(1)}, f32[1,1,2,128,128]{4,3,2,1,0:T(8,128)S(1)}, u32[]{:S(2)}, u32[]{:S(2)}) collective-permute-start(f32[1,1,2,128,128]{4,3,2,1,0:T(8,128)S(1)} %get-tuple-element.34), channel_id=1, source_target_pairs={{0,1},{1,0},{2,3},{3,2},{4,8},{5,9},{6,10},{7,11},{8,4},{9,5},{10,... | collective-permute-start | bytes 393224 | tf_op jit(solution)/shard_map/ppermute | solution.py:206
  12.9 0.0 collective-permute-done.1.even_ref
  12.9 0.0 collective-permute-done.odd_ref
  12.9 2.0 %shard_map.58 = (f32[1,1,2,128,128]{4,3,2,1,0:T(8,128)S(1)}, f32[2,1,2,128,128]{4,3,2,1,0:T(8,128)S(1)}, f32[2,1,2,128,128]{4,3,2,1,0:T(8,128)S(1)}) custom-call(f32[1,1,2,128,128]{4,3,2,1,0:T(8,128)S(1)} %get-tuple-element.22.own_ref, f32[1,1,2,128,128]{4,3,2,1,0:T(8,128)S(1)} %collective-permute-done.odd_ref, ...), custom_call_target="tpu_custom_call" | custom-call | flops 10000000000 | tf_op jit(solution)/shard_map/pallas_call | solution.py:215
  14.9 0.5 %collective-permute-start.5 = (f32[1,1,2,128,128]{4,3,2,1,0:T(8,128)S(1)}, f32[1,1,2,128,128]{4,3,2,1,0:T(8,128)S(1)}, u32[]{:S(2)}, u32[]{:S(2)}) collective-permute-start(f32[1,1,2,128,128]{4,3,2,1,0:T(8,128)S(1)} %get-tuple-element.35), channel_id=1, source_target_pairs={{0,1},{1,0},{2,3},{3,2},{4,8},{5,9},{6,10},{7,11},{8,4},{9,5},{10,... | collective-permute-start | bytes 393224 | tf_op jit(solution)/shard_map/ppermute | solution.py:206
  15.3 0.0 collective-permute-start.6
  15.3 0.5 %collective-permute-done.4.got_first_ref = f32[1,1,2,128,128]{4,3,2,1,0:T(8,128)S(1)} collective-permute-done((f32[1,1,2,128,128]{4,3,2,1,0:T(8,128)S(1)}, f32[1,1,2,128,128]{4,3,2,1,0:T(8,128)S(1)}, u32[]{:S(2)}, u32[]{:S(2)}) %collective-permute-start.4) | collective-permute-done | bytes 131104 | tf_op jit(solution)/shard_map/ppermute | solution.py:206
  15.9 4.0 %collective-permute-done.5.got_rest_ref = f32[1,1,2,128,128]{4,3,2,1,0:T(8,128)S(1)} collective-permute-done((f32[1,1,2,128,128]{4,3,2,1,0:T(8,128)S(1)}, f32[1,1,2,128,128]{4,3,2,1,0:T(8,128)S(1)}, u32[]{:S(2)}, u32[]{:S(2)}) %collective-permute-start.5) | collective-permute-done | bytes 131104 | tf_op jit(solution)/shard_map/ppermute | solution.py:206
  19.9 0.0 collective-permute-done.6.got_even_ref
  19.9 0.8 %shard_map.60 = f32[2,1,2,128,128]{4,3,2,1,0:T(8,128)} custom-call(f32[2,1,2,128,128]{4,3,2,1,0:T(8,128)S(1)} %shard_map.59.stay_ref, f32[1,1,2,128,128]{4,3,2,1,0:T(8,128)S(1)} %collective-permute-done.5.got_rest_ref, f32[2,1,2,128,128]{4,3,2,1,0:T(8,128)S(1)} %collective-permute-done.6.got_even_ref), custom_call_target="tpu_custom_call" | custom-call | flops 1000000000 | tf_op jit(solution)/shard_map/pallas_call | solution.py:215
  (8 shorter events, 0.1 us)
Async XLA Ops:
  0.0 1.0 %copy-start = (f32[2,1,2,128,128]{4,3,2,1,0:T(8,128)S(1)}, f32[2,1,2,128,128]{4,3,2,1,0:T(8,128)}, u32[]{:S(2)}) copy-start(f32[2,1,2,128,128]{4,3,2,1,0:T(8,128)} %param.5) | copy-start | bytes 786436
  1.0 3.2 %copy-start.1 = (f32[4,1,3,2,128,128]{5,4,3,2,1,0:T(8,128)S(1)}, f32[4,1,3,2,128,128]{5,4,3,2,1,0:T(8,128)}, u32[]{:S(2)}) copy-start(f32[4,1,3,2,128,128]{5,4,3,2,1,0:T(8,128)} %couple_ref.1) | copy-start | bytes 4718596
  1.0 3.2 %copy-start.2 = (s32[4]{0:T(128)S(1)}, s32[4]{0:T(128)}, u32[]{:S(2)}) copy-start(s32[4]{0:T(128)} %shifts_hbm.1) | copy-start | bytes 52
  1.0 3.2 %copy-start.3 = (f32[4]{0:T(128)S(1)}, f32[4]{0:T(128)}, u32[]{:S(2)}) copy-start(f32[4]{0:T(128)} %occupation_hbm.1) | copy-start | bytes 52
  1.0 3.2 %copy-start.4 = (s32[1,3]{1,0:T(1,128)S(1)}, s32[1,3]{1,0:T(1,128)}, u32[]{:S(2)}) copy-start(s32[1,3]{1,0:T(1,128)} %neighbours_hbm.1) | copy-start | bytes 40
  1.0 7.1 %collective-permute-start.3 = (f32[1,1,2,128,128]{4,3,2,1,0:T(8,128)S(1)}, f32[1,1,2,128,128]{4,3,2,1,0:T(8,128)S(1)}, u32[]{:S(2)}, u32[]{:S(2)}) collective-permute-start(f32[1,1,2,128,128]{4,3,2,1,0:T(8,128)S(1)} %shard_map.55.own_ref), channel_id=1, source_target_pairs={{0,1},{1,0},{2,3},{3,2},{4,5},{5,4},{6,7},{7,6},{8,9},{9,8},{10,11... | collective-permute-start | bytes 393224 | tf_op jit(solution)/shard_map/ppermute | solution.py:206
  4.1 4.0 %collective-permute-start.2 = (f32[1,1,2,128,128]{4,3,2,1,0:T(8,128)S(1)}, f32[1,1,2,128,128]{4,3,2,1,0:T(8,128)S(1)}, u32[]{:S(2)}, u32[]{:S(2)}) collective-permute-start(f32[1,1,2,128,128]{4,3,2,1,0:T(8,128)S(1)} %shard_map.55.own_ref), channel_id=1, source_target_pairs={{0,4},{1,2},{2,1},{3,7},{4,0},{5,6},{6,5},{7,3},{8,12},{9,10},{10,... | collective-permute-start | bytes 393224 | tf_op jit(solution)/shard_map/ppermute | solution.py:206
  4.9 8.0 %collective-permute-start.1 = (f32[1,1,2,128,128]{4,3,2,1,0:T(8,128)S(1)}, f32[1,1,2,128,128]{4,3,2,1,0:T(8,128)S(1)}, u32[]{:S(2)}, u32[]{:S(2)}) collective-permute-start(f32[1,1,2,128,128]{4,3,2,1,0:T(8,128)S(1)} %get-tuple-element.22.own_ref), channel_id=1, source_target_pairs={{0,1},{1,0},{2,3},{3,2},{4,5},{5,4},{6,7},{7,6},{8,9},{9,8},{10,11... | collective-permute-start | bytes 393224 | tf_op jit(solution)/shard_map/ppermute | solution.py:206
  8.1 4.8 %collective-permute-start = (f32[1,1,2,128,128]{4,3,2,1,0:T(8,128)S(1)}, f32[1,1,2,128,128]{4,3,2,1,0:T(8,128)S(1)}, u32[]{:S(2)}, u32[]{:S(2)}) collective-permute-start(f32[1,1,2,128,128]{4,3,2,1,0:T(8,128)S(1)} %get-tuple-element.22.own_ref), channel_id=1, source_target_pairs={{0,4},{1,2},{2,1},{3,7},{4,0},{5,6},{6,5},{7,3},{8,12},{9,10},{10,... | collective-permute-start | bytes 393224 | tf_op jit(solution)/shard_map/ppermute | solution.py:206
  10.1 5.7 %collective-permute-start.4 = (f32[1,1,2,128,128]{4,3,2,1,0:T(8,128)S(1)}, f32[1,1,2,128,128]{4,3,2,1,0:T(8,128)S(1)}, u32[]{:S(2)}, u32[]{:S(2)}) collective-permute-start(f32[1,1,2,128,128]{4,3,2,1,0:T(8,128)S(1)} %get-tuple-element.34), channel_id=1, source_target_pairs={{0,1},{1,0},{2,3},{3,2},{4,8},{5,9},{6,10},{7,11},{8,4},{9,5},{10,... | collective-permute-start | bytes 393224 | tf_op jit(solution)/shard_map/ppermute | solution.py:206
  14.9 5.0 %collective-permute-start.5 = (f32[1,1,2,128,128]{4,3,2,1,0:T(8,128)S(1)}, f32[1,1,2,128,128]{4,3,2,1,0:T(8,128)S(1)}, u32[]{:S(2)}, u32[]{:S(2)}) collective-permute-start(f32[1,1,2,128,128]{4,3,2,1,0:T(8,128)S(1)} %get-tuple-element.35), channel_id=1, source_target_pairs={{0,1},{1,0},{2,3},{3,2},{4,8},{5,9},{6,10},{7,11},{8,4},{9,5},{10,... | collective-permute-start | bytes 393224 | tf_op jit(solution)/shard_map/ppermute | solution.py:206
  15.3 4.6 %collective-permute-start.6 = (f32[2,1,2,128,128]{4,3,2,1,0:T(8,128)S(1)}, f32[2,1,2,128,128]{4,3,2,1,0:T(8,128)S(1)}, u32[]{:S(2)}, u32[]{:S(2)}) collective-permute-start(f32[2,1,2,128,128]{4,3,2,1,0:T(8,128)S(1)} %get-tuple-element.36), channel_id=1, source_target_pairs={{0,4},{1,5},{2,6},{3,7},{4,0},{5,1},{6,2},{7,3},{8,12},{9,13},{10,... | collective-permute-start | bytes 786440 | tf_op jit(solution)/shard_map/ppermute | solution.py:206
